TPU v7x, 512 devices: a whole 4x8x8 slice. The times are simulated.
512 devices in a mesh: dp: 16 (over z, y_hi), ep: 32 (over y_lo, x, core).
Axes of the slice: x: 4, y: 8 (y_hi: 2, y_lo: 4; y = y_hi * 4 + y_lo), z: 8, core: 2. Of those that a mesh axis runs over, the one named last changes fastest.
Arguments:
- tokens: bfloat16 [16384, 2048], P(('dp', 'ep')), may hold values from -6 to 6
- grad_out: bfloat16 [16384, 2048], P(('dp', 'ep')), may hold values from -6 to 6
- expert_ids: int32 [16384, 2], P(('dp', 'ep')), may hold values from 0 to 7, all different within a row; in each aligned block of 32 rows (0 to 31, 32 to 63, ...) at most 9 rows name the same one
- combine: float32 [16384, 2], P(('dp', 'ep')), may hold values from 0.2 to 1
- w_gate: bfloat16 [32, 2048, 768], P('ep', 'dp'), may hold values from -0.125 to 0.125
- w_up: bfloat16 [32, 2048, 768], P('ep', 'dp'), may hold values from -0.125 to 0.125
- w_down: bfloat16 [32, 768, 2048], P('ep', None, 'dp'), may hold values from -0.109375 to 0.109375
Outputs:
- layer_out: bfloat16 [16384, 2048], P(('dp', 'ep'))
- grad_tokens: bfloat16 [16384, 2048], P(('dp', 'ep'))
- grad_gate: bfloat16 [32, 2048, 768], P('ep', 'dp')
Inputs may be any that keep to these rules, and one draw needn't show every extreme that they name: `expert_ids`: in each aligned block of 32 rows (the rows of one device) no expert is named by more than 9 rows, a bound that some block reaches; the two ids of a row differ.
All inputs are finite; a program needn't handle non-finite values.
Results may differ from a plain program's by a relative error of at most 0.02.
Values may be sent and summed in bfloat16 or wider, within the bound.
No kernel may reach another device: no remote copies, remote signals or barrier semaphores. Data moves between devices by JAX's collectives and lax.ppermute only.
A program may use at most 64 MiB of HBM per device.

v0:
```python
import jax
import jax.numpy as jnp
from jax import lax
from jax.sharding import PartitionSpec as P

EXPERTS = 8
CAP = 9


def per_device(tokens, grad_out, expert_ids, combine, w_gate, w_up, w_down):
    ep_count = lax.axis_size("ep")
    share_count = ep_count // EXPERTS
    token_count = tokens.shape[0]
    model_dim = tokens.shape[1]
    hidden_dim = w_gate.shape[2]
    paired_ids = expert_ids.reshape(-1)
    one_hot = (paired_ids[:, None] == jnp.arange(EXPERTS, dtype=jnp.int32)[None, :]).astype(
        jnp.int32
    )
    earlier_count = jnp.cumsum(one_hot, axis=0) - one_hot
    position = jnp.sum(earlier_count * one_hot, axis=1)
    target = paired_ids * CAP + position
    slot_hit = target[None, :] == jnp.arange(EXPERTS * CAP, dtype=jnp.int32)[:, None]
    pick_pairs = slot_hit.astype(jnp.bfloat16)
    pick_tokens = jnp.any(slot_hit.reshape(EXPERTS * CAP, token_count, 2), axis=2).astype(
        jnp.bfloat16
    )
    routed_in = jnp.dot(pick_tokens, tokens, preferred_element_type=jnp.float32).astype(
        jnp.bfloat16
    )
    scaled = (combine[:, :, None] * grad_out[:, None, :].astype(jnp.float32)).astype(jnp.bfloat16)
    scaled = scaled.reshape(token_count * 2, model_dim)
    routed_grad = jnp.dot(pick_pairs, scaled, preferred_element_type=jnp.float32).astype(
        jnp.bfloat16
    )

    def spread_out(values):
        wide = jnp.broadcast_to(
            values.reshape(EXPERTS, 1, CAP, model_dim), (EXPERTS, share_count, CAP, model_dim)
        )
        return wide.reshape(ep_count, CAP, model_dim)

    recv_in, recv_grad = (
        lax.all_to_all(spread_out(routed_in), "ep", split_axis=0, concat_axis=0, tiled=True),
        lax.all_to_all(spread_out(routed_grad), "ep", split_axis=0, concat_axis=0, tiled=True),
    )
    row_total = ep_count * CAP
    expert_in = recv_in.reshape(row_total, model_dim)
    expert_grad = recv_grad.reshape(row_total, model_dim)
    paired_rows = jnp.concatenate([w_gate[0], w_up[0]], axis=1)
    down_rows = w_down[0]
    contract_last = (((1,), (1,)), ((), ()))
    paired_all, down_all = (
        lax.all_gather(paired_rows, "dp", axis=0, tiled=True),
        lax.all_gather(down_rows, "dp", axis=1, tiled=True),
    )
    both_pre = jnp.dot(expert_in, paired_all, preferred_element_type=jnp.float32)
    grad_hidden = lax.dot_general(
        expert_grad, down_all, contract_last, preferred_element_type=jnp.float32
    )
    gate_pre = both_pre[:, :hidden_dim]
    up_pre = both_pre[:, hidden_dim:]
    sigma = jax.nn.sigmoid(gate_pre)
    hidden_act = (gate_pre * sigma * up_pre).astype(jnp.bfloat16)
    grad_upper = (grad_hidden * gate_pre * sigma).astype(jnp.bfloat16)
    grad_gated = (grad_hidden * up_pre * sigma * (1.0 + gate_pre * (1.0 - sigma))).astype(
        jnp.bfloat16
    )
    grad_paired = jnp.concatenate([grad_gated, grad_upper], axis=1)
    out_rows = jnp.dot(hidden_act, down_all, preferred_element_type=jnp.float32).astype(
        jnp.bfloat16
    )
    back_rows = lax.dot_general(
        grad_paired, paired_all, contract_last, preferred_element_type=jnp.float32
    ).astype(jnp.bfloat16)
    summed = lax.psum_scatter(
        lax.dot_general(
            expert_in, grad_gated, (((0,), (0,)), ((), ())), preferred_element_type=jnp.float32
        ).astype(jnp.bfloat16),
        "dp",
        scatter_dimension=0,
        tiled=True,
    )
    grad_gate = summed[None]
    returned, returned_out = (
        lax.all_to_all(
            back_rows.reshape(ep_count, CAP, model_dim),
            "ep",
            split_axis=0,
            concat_axis=0,
            tiled=True,
        ),
        lax.all_to_all(
            out_rows.reshape(ep_count, CAP, model_dim),
            "ep",
            split_axis=0,
            concat_axis=0,
            tiled=True,
        ),
    )
    per_expert = jnp.sum(
        returned.reshape(EXPERTS, share_count, CAP, model_dim).astype(jnp.float32), axis=1
    )
    per_expert = per_expert.reshape(EXPERTS * CAP, model_dim)
    per_expert_out = jnp.sum(
        returned_out.reshape(EXPERTS, share_count, CAP, model_dim).astype(jnp.float32), axis=1
    )
    per_expert_out = per_expert_out.reshape(EXPERTS * CAP, model_dim)
    slot_float = slot_hit.astype(jnp.float32)
    pair_grads = lax.dot_general(
        slot_float,
        per_expert,
        (((0,), (0,)), ((), ())),
        precision=lax.Precision.HIGHEST,
        preferred_element_type=jnp.float32,
    )
    pair_outs = lax.dot_general(
        slot_float,
        per_expert_out,
        (((0,), (0,)), ((), ())),
        precision=lax.Precision.HIGHEST,
        preferred_element_type=jnp.float32,
    )
    grad_tokens = jnp.sum(pair_grads.reshape(token_count, 2, model_dim), axis=1).astype(
        jnp.bfloat16
    )
    layer_out = jnp.sum(
        pair_outs.reshape(token_count, 2, model_dim) * combine[:, :, None], axis=1
    ).astype(jnp.bfloat16)
    return (layer_out, grad_tokens, grad_gate)


def solution(mesh):
    placed = (
        P(("dp", "ep"), None),
        P(("dp", "ep"), None),
        P(("dp", "ep"), None),
        P(("dp", "ep"), None),
        P("ep", "dp", None),
        P("ep", "dp", None),
        P("ep", None, "dp"),
    )
    return jax.shard_map(
        per_device,
        mesh=mesh,
        in_specs=placed,
        out_specs=(P(("dp", "ep"), None), P(("dp", "ep"), None), P("ep", "dp", None)),
        check_vma=False,
    )
```

profile of v0, /device:TPU:8, one launch (start us, length us, event | category | flops | bytes accessed | tf_op | source)
XLA Modules:
  0.0 590.1 jit_solution(6709142406357131259)
XLA Ops:
  7.2 1.8 pad_maximum_fusion
  12.5 1.6 broadcast_in_dim.11
  14.0 9.7 %all-to-all-start = ((bf16[32,9,2048]{2,1,0:T(8,128)(2,1)}), bf16[32,9,2048]{2,1,0:T(8,128)(2,1)S(1)}, u32[]{:S(2)}, u32[]{:S(2)}) async-start(bf16[32,9,2048]{2,1,0:T(8,128)(2,1)} %bitcast.1), calls=%async_computation | async-start | bytes 4194304 | tf_op jit(solution)/shard_map/all_to_all | solution.py:44
  25.0 53.7 %all-to-all-done = bf16[32,9,2048]{2,1,0:T(8,128)(2,1)S(1)} async-done(((bf16[32,9,2048]{2,1,0:T(8,128)(2,1)}), bf16[32,9,2048]{2,1,0:T(8,128)(2,1)S(1)}, u32[]{:S(2)}, u32[]{:S(2)}) %all-to-all-start) | async-done | bytes 1179680 | tf_op jit(solution)/shard_map/all_to_all | solution.py:44
  78.7 1.7 broadcast_in_dim.26
  80.4 7.9 %all-to-all-start.2 = ((bf16[32,9,2048]{2,1,0:T(8,128)(2,1)}), bf16[32,9,2048]{2,1,0:T(8,128)(2,1)}, u32[]{:S(2)}, u32[]{:S(2)}) async-start(bf16[32,9,2048]{2,1,0:T(8,128)(2,1)} %bitcast.6), calls=%async_computation.2 | async-start | bytes 4194304 | tf_op jit(solution)/shard_map/all_to_all | solution.py:45
  89.0 112.9 %all-to-all-done.2 = bf16[32,9,2048]{2,1,0:T(8,128)(2,1)} async-done(((bf16[32,9,2048]{2,1,0:T(8,128)(2,1)}), bf16[32,9,2048]{2,1,0:T(8,128)(2,1)}, u32[]{:S(2)}, u32[]{:S(2)}) %all-to-all-start.2) | async-done | bytes 1179680 | tf_op jit(solution)/shard_map/all_to_all | solution.py:45
  201.9 1.8 reshape.99
  203.7 1.7 all-gather.4.cloned.1.call-done
  205.4 6.0 %fusion.23 = f32[288,1536]{1,0:T(8,128)} fusion(bf16[288,2048]{1,0:T(8,128)(2,1)S(1)} %reshape.95, bf16[2048,1536]{1,0:T(8,128)(2,1)} %all-gather.4.cloned.1.call-done), kind=kOutput, calls=%fused_computation.40 | convolution fusion | flops 1811939328 | bytes 9240576 | tf_op jit(solution)/shard_map/dot_general | solution.py:57
  211.4 127.0 %all-gather.6.cloned.1.call-done = bf16[1,768,2048]{2,1,0:T(8,128)(2,1)} async-done(((bf16[1,768,128]{2,1,0:T(8,128)(2,1)}), bf16[1,768,2048]{2,1,0:T(8,128)(2,1)}) %all-gather.6.cloned.1.call-update) | async-done | bytes 3145744 | tf_op jit(solution)/shard_map/all_gather | solution.py:55
  338.5 3.7 multiply_convert_fusion.1
  342.2 3.5 convolution_convert_fusion
  345.7 4.8 convolution_convert_fusion.1
  350.5 1.6 reshape.100
  352.1 6.5 %all-to-all-start.3 = ((bf16[32,9,2048]{2,1,0:T(8,128)(2,1)}), bf16[32,9,2048]{2,1,0:T(8,128)(2,1)S(1)}, u32[]{:S(2)}, u32[]{:S(2)}) async-start(bf16[32,9,2048]{2,1,0:T(8,128)(2,1)} %reshape.100), calls=%async_computation.3 | async-start | bytes 4194304 | tf_op jit(solution)/shard_map/all_to_all | solution.py:86
  358.6 3.5 fusion.4
  362.1 1.6 reshape.96
  363.7 49.0 %all-to-all-done.3 = bf16[32,9,2048]{2,1,0:T(8,128)(2,1)S(1)} async-done(((bf16[32,9,2048]{2,1,0:T(8,128)(2,1)}), bf16[32,9,2048]{2,1,0:T(8,128)(2,1)S(1)}, u32[]{:S(2)}, u32[]{:S(2)}) %all-to-all-start.3) | async-done | bytes 1179680 | tf_op jit(solution)/shard_map/all_to_all | solution.py:86
  412.7 7.1 %all-to-all-start.1 = ((bf16[32,9,2048]{2,1,0:T(8,128)(2,1)}), bf16[32,9,2048]{2,1,0:T(8,128)(2,1)}, u32[]{:S(2)}, u32[]{:S(2)}) async-start(bf16[32,9,2048]{2,1,0:T(8,128)(2,1)} %reshape.96), calls=%async_computation.1 | async-start | bytes 4194304 | tf_op jit(solution)/shard_map/all_to_all | solution.py:93
  420.2 58.2 %all-to-all-done.1 = bf16[32,9,2048]{2,1,0:T(8,128)(2,1)} async-done(((bf16[32,9,2048]{2,1,0:T(8,128)(2,1)}), bf16[32,9,2048]{2,1,0:T(8,128)(2,1)}, u32[]{:S(2)}, u32[]{:S(2)}) %all-to-all-start.1) | async-done | bytes 1179680 | tf_op jit(solution)/shard_map/all_to_all | solution.py:93
  478.5 2.1 convert_reduce_fusion.1
  481.8 1.1 fusion.7
  482.8 100.7 %reduce-scatter.2.cloned.1.call-done = bf16[128,768]{1,0:T(8,128)(2,1)} async-done(((bf16[2048,768]{1,0:T(8,128)(2,1)}), bf16[128,768]{1,0:T(8,128)(2,1)}) %reduce-scatter.2.cloned.1.call-update) | async-done | bytes 196624 | tf_op jit(solution)/shard_map/reduce_scatter | solution.py:76
  (35 shorter events, 6.8 us)
Async XLA Ops:
  7.2 4.9 copy-start
  7.2 198.3 %all-gather.4.cloned.1.call-start = ((), (), s32[]{:S(2)}) async-start(), calls=%async_computation.5 | async-start | bytes 6684672 | tf_op jit(solution)/shard_map/all_gather | solution.py:54
  9.1 329.4 %all-gather.6.cloned.1.call-start = ((), (), s32[]{:S(2)}) async-start(), calls=%async_computation.7 | async-start | bytes 3342336 | tf_op jit(solution)/shard_map/all_gather | solution.py:55
  14.0 9.7 %copy-start.1 = (bf16[32,2048]{1,0:T(8,128)(2,1)S(1)}, bf16[32,2048]{1,0:T(8,128)(2,1)}, u32[]{:S(2)}) copy-start(bf16[32,2048]{1,0:T(8,128)(2,1)} %param.8) | copy-start | bytes 393220
  14.0 10.3 %copy-start.2 = (f32[32,2]{0,1:T(2,128)S(1)}, f32[32,2]{0,1:T(2,128)}, u32[]{:S(2)}) copy-start(f32[32,2]{0,1:T(2,128)} %param.10) | copy-start | bytes 772
  14.0 64.7 %all-to-all-start = ((bf16[32,9,2048]{2,1,0:T(8,128)(2,1)}), bf16[32,9,2048]{2,1,0:T(8,128)(2,1)S(1)}, u32[]{:S(2)}, u32[]{:S(2)}) async-start(bf16[32,9,2048]{2,1,0:T(8,128)(2,1)} %bitcast.1), calls=%async_computation | async-start | bytes 4194304 | tf_op jit(solution)/shard_map/all_to_all | solution.py:44
  80.4 121.5 %all-to-all-start.2 = ((bf16[32,9,2048]{2,1,0:T(8,128)(2,1)}), bf16[32,9,2048]{2,1,0:T(8,128)(2,1)}, u32[]{:S(2)}, u32[]{:S(2)}) async-start(bf16[32,9,2048]{2,1,0:T(8,128)(2,1)} %bitcast.6), calls=%async_computation.2 | async-start | bytes 4194304 | tf_op jit(solution)/shard_map/all_to_all | solution.py:45
  88.3 495.2 %reduce-scatter.2.cloned.1.call-start = ((), (), s32[]{:S(2)}) async-start(), calls=%async_computation.6 | async-start | bytes 3342336 | tf_op jit(solution)/shard_map/reduce_scatter | solution.py:76
  352.1 60.6 %all-to-all-start.3 = ((bf16[32,9,2048]{2,1,0:T(8,128)(2,1)}), bf16[32,9,2048]{2,1,0:T(8,128)(2,1)S(1)}, u32[]{:S(2)}, u32[]{:S(2)}) async-start(bf16[32,9,2048]{2,1,0:T(8,128)(2,1)} %reshape.100), calls=%async_computation.3 | async-start | bytes 4194304 | tf_op jit(solution)/shard_map/all_to_all | solution.py:86
  412.7 65.8 %all-to-all-start.1 = ((bf16[32,9,2048]{2,1,0:T(8,128)(2,1)}), bf16[32,9,2048]{2,1,0:T(8,128)(2,1)}, u32[]{:S(2)}, u32[]{:S(2)}) async-start(bf16[32,9,2048]{2,1,0:T(8,128)(2,1)} %reshape.96), calls=%async_computation.1 | async-start | bytes 4194304 | tf_op jit(solution)/shard_map/all_to_all | solution.py:93
Sparse Core Ops, SparseCore 0:
  11.2 194.2 all-gather.3
  208.5 129.9 all-gather.5
  345.8 237.6 reduce-scatter.1
where the time goes:
time: 591 us; the launch traced here: 590 us
  waiting for transfers between devices  504 us (85%)
  starting transfers between devices  31.2 us (5%)
  matrix products  24.3 us (4%)
  between operations  14 us (2%)
  local copies, waits for them, and re-layouts  11 us (2%)
    all_gather x1, waiting for transfers between devices, per_device(): lax.all_gather(down_rows, 'dp', axis=1, tiled=True)  127 us
    all_to_all x1, waiting for transfers between devices, per_device(): lax.all_to_all(spread_out(routed_grad), 'ep', split_axis=0, concat_axis=0...  113 us
    reduce_scatter x1, waiting for transfers between devices, per_device(): lax.psum_scatter(lax.dot_general(expert_in, grad_gated, (((0,), (0,)), ((...  101 us
    all_to_all x1, waiting for transfers between devices, per_device(): lax.all_to_all(out_rows.reshape(ep_count, CAP, model_dim), 'ep', split_ax...  58.2 us
    all_to_all x1, waiting for transfers between devices, per_device(): lax.all_to_all(spread_out(routed_in), 'ep', split_axis=0, concat_axis=0,...  53.7 us
    all_to_all x1, waiting for transfers between devices, per_device(): lax.all_to_all(back_rows.reshape(ep_count, CAP, model_dim), 'ep', split_a...  49 us
  transfers between devices with their start and end apart: 7, of which 7 were waited for; matrix products, arithmetic and copies ran while one was open for 5% of the time, Pallas kernels for 0%

commit v1 on v0

v1 whole, which is shorter than its diff:
```python
import jax
import jax.numpy as jnp
from jax import lax
from jax.experimental import pallas as pl
from jax.experimental.pallas import tpu as pltpu
from jax.sharding import Mesh, PartitionSpec as P

EXPERTS = 8
CAP = 9
NZ = 8
AXES = ("z", "h", "y", "x", "c")
EP = ("y", "x", "c")
RIGHT = [(i, (i + 1) % NZ) for i in range(NZ)]
LEFT = [(i, (i - 1) % NZ) for i in range(NZ)]
SWAP = [(0, 1), (1, 0)]
BF = jnp.bfloat16
F32 = jnp.float32
VMEM_LIMIT = 60 * 1024 * 1024
ROWS = 288
D = 2048
HID = 768


def load_pieces(pieces, w_ref, sems):
    copies = [
        pltpu.make_async_copy(p, w_ref.at[pl.ds(i * 128, 128), :], sems.at[i])
        for i, p in enumerate(pieces)
    ]
    for c in copies:
        c.start()
    for c in copies:
        c.wait()


def hidden_kernel(x_ref, y_ref, *refs):
    pieces, h_ref, d_ref, gg, w_ref, sems = refs[:16], refs[16], refs[17], refs[18:34], refs[34], refs[35]
    load_pieces(pieces, w_ref, sems)
    x = x_ref[...]
    y = y_ref[...]
    for n in range(HID // 256):
        at = n * 256
        g = jnp.dot(x, w_ref[:, at : at + 256], preferred_element_type=F32)
        u = jnp.dot(x, w_ref[:, HID + at : HID + at + 256], preferred_element_type=F32)
        dh = jnp.dot(y, w_ref[:, 2 * HID + at : 2 * HID + at + 256], preferred_element_type=F32)
        s = 1.0 / (1.0 + jnp.exp(-g))
        gs = g * s
        h_ref[:, at : at + 256] = (gs * u).astype(BF)
        d_ref[:, HID + at : HID + at + 256] = (dh * gs).astype(BF)
        d_ref[:, at : at + 256] = (dh * u * s * (1.0 + g * (1.0 - s))).astype(BF)
    dg = d_ref[:, :HID]
    for i in range(16):
        gg[i][...] = lax.dot_general(
            x_ref[:, i * 128 : (i + 1) * 128], dg, (((0,), (0,)), ((), ())), preferred_element_type=F32
        ).astype(BF)


def rows_kernel(h_ref, d_ref, *refs):
    pieces, out_ref, back_ref, w_ref, sems = refs[:16], refs[16], refs[17], refs[18], refs[19]
    load_pieces(pieces, w_ref, sems)
    last = (((1,), (1,)), ((), ()))
    for n in range(D // 256):
        at = n * 256
        back_ref[:, at : at + 256] = lax.dot_general(
            d_ref[...], w_ref[at : at + 256, : 2 * HID], last, preferred_element_type=F32
        ).astype(BF)
        out_ref[:, at : at + 256] = lax.dot_general(
            h_ref[...], w_ref[at : at + 256, 2 * HID :], last, preferred_element_type=F32
        ).astype(BF)


VM = pl.BlockSpec(memory_space=pltpu.VMEM)
ANY = pl.BlockSpec(memory_space=pl.ANY)


def hidden_call(x, y, pieces):
    res = pl.pallas_call(
        hidden_kernel,
        out_shape=[
            jax.ShapeDtypeStruct((ROWS, HID), BF),
            jax.ShapeDtypeStruct((ROWS, 2 * HID), BF),
        ]
        + [jax.ShapeDtypeStruct((128, HID), BF)] * 16,
        in_specs=[VM, VM] + [ANY] * 16,
        out_specs=[VM] * 18,
        scratch_shapes=[pltpu.VMEM((D, 3 * HID), BF), pltpu.SemaphoreType.DMA((16,))],
        compiler_params=pltpu.CompilerParams(vmem_limit_bytes=VMEM_LIMIT),
        cost_estimate=pl.CostEstimate(flops=2 * ROWS * D * HID * 4, bytes_accessed=17_000_000, transcendentals=ROWS * HID),
    )(x, y, *pieces)
    return res[0], res[1], res[2:]


def rows_call(h, d, pieces):
    return pl.pallas_call(
        rows_kernel,
        out_shape=[jax.ShapeDtypeStruct((ROWS, D), BF)] * 2,
        in_specs=[VM, VM] + [ANY] * 16,
        out_specs=[VM] * 2,
        scratch_shapes=[pltpu.VMEM((D, 3 * HID), BF), pltpu.SemaphoreType.DMA((16,))],
        compiler_params=pltpu.CompilerParams(vmem_limit_bytes=VMEM_LIMIT),
        cost_estimate=pl.CostEstimate(flops=2 * ROWS * D * HID * 3, bytes_accessed=14_000_000, transcendentals=0),
    )(h, d, *pieces)


def right(v):
    return lax.ppermute(v, "z", RIGHT)


def left(v):
    return lax.ppermute(v, "z", LEFT)


def add(a, b):
    return (a.astype(F32) + b.astype(F32)).astype(BF)


def to_relative(v, z, h):
    rolled = lax.dynamic_slice(jnp.concatenate([v, v], axis=1), (0, z * 256), v.shape)
    parts = rolled.reshape(v.shape[0], NZ, 2, 128)
    return jnp.where(h == 1, parts[:, :, ::-1], parts).reshape(v.shape)


def from_relative(v, z, h):
    parts = v.reshape(v.shape[0], NZ, 2, 128)
    parts = jnp.where(h == 1, parts[:, :, ::-1], parts).reshape(v.shape)
    return lax.dynamic_slice(jnp.concatenate([parts, parts], axis=1), (0, (NZ - z) * 256), v.shape)


def per_device(tokens, grad_out, expert_ids, combine, w_gate, w_up, w_down):
    z, h = lax.axis_index("z"), lax.axis_index("h")
    own = jnp.concatenate([w_gate[0], w_up[0], w_down[0].T], axis=1)
    a, b = [None] * NZ, [None] * NZ
    a[0] = own
    b[0] = lax.ppermute(own, "h", SWAP)
    for s in range(1, 5):
        a[NZ - s] = right(a[(NZ - s + 1) % NZ])
        if s < 4:
            a[s] = left(a[s - 1])
    for s in range(1, 5):
        if s < 4:
            b[NZ - s] = right(b[(NZ - s + 1) % NZ])
        b[s] = left(b[s - 1])
    pieces = [v for pair in zip(a, b) for v in pair]

    e0, e1 = expert_ids[:, 0], expert_ids[:, 1]
    before = jnp.arange(32)[None, :] < jnp.arange(32)[:, None]

    def count(mine):
        hit = (e0[None, :] == mine[:, None]).astype(jnp.int32) + (e1[None, :] == mine[:, None]).astype(jnp.int32)
        return jnp.sum(jnp.where(before, hit, 0), axis=1)

    t0, t1 = e0 * CAP + count(e0), e1 * CAP + count(e1)
    slots = jnp.arange(EXPERTS * CAP, dtype=jnp.int32)[:, None]
    hit0, hit1 = slots == t0[None, :], slots == t1[None, :]
    pick = (hit0 | hit1).astype(BF)
    scale = jnp.sum(
        jnp.where(hit0, combine[:, 0][None, :], 0.0) + jnp.where(hit1, combine[:, 1][None, :], 0.0), axis=1
    )
    both = jnp.concatenate([to_relative(tokens, z, h), to_relative(grad_out, z, h)], axis=1)
    picked = jnp.dot(pick, both, preferred_element_type=F32)
    routed_x = picked[:, :D].astype(BF)
    routed_y = (picked[:, D:] * scale[:, None]).astype(BF)

    def fold(v, lead):
        return v.reshape(lead, CAP, 8, 256)

    payload = jnp.concatenate([fold(routed_x, EXPERTS), fold(routed_y, EXPERTS)], axis=1)
    payload = jnp.broadcast_to(payload[:, None], (EXPERTS, 4, 2 * CAP, 8, 256)).reshape(32, 2 * CAP, 8, 256)
    got = lax.all_to_all(payload, EP, 0, 0, tiled=True)
    x = got[:, :CAP].reshape(ROWS, D)
    y = got[:, CAP:].reshape(ROWS, D)

    hid, dgu, gg = hidden_call(x, y, pieces)

    mine, other = gg[0::2], gg[1::2]
    r, l = other[3], other[4]
    for s in range(1, 5):
        if s < 4:
            r = right(r)
            if s < 3:
                r = add(r, other[3 - s])
        l = left(l)
        if s < 4:
            l = add(l, other[4 + s])
    other_sum = (r.astype(F32) + l.astype(F32) + other[0].astype(F32)).astype(BF)
    crossed = lax.ppermute(other_sum, "h", SWAP)
    r, l = mine[4], mine[5]
    for s in range(1, 5):
        r = right(r)
        if s < 4:
            r = add(r, mine[4 - s])
            l = left(l)
            if s < 3:
                l = add(l, mine[5 + s])
    grad_gate = (r.astype(F32) + l.astype(F32) + mine[0].astype(F32) + crossed.astype(F32)).astype(BF)[None]

    out_rows, back_rows = rows_call(hid, dgu, pieces)
    payload = jnp.concatenate([fold(out_rows, 32), fold(back_rows, 32)], axis=1)
    got = lax.all_to_all(payload, EP, 0, 0, tiled=True)
    total = jnp.sum(got.reshape(EXPERTS, 4, 2 * CAP, 8, 256).astype(F32), axis=1)
    sum_out = total[:, :CAP].reshape(EXPERTS * CAP, D) * scale[:, None]
    sum_back = total[:, CAP:].reshape(EXPERTS * CAP, D)
    place = (hit0 | hit1).astype(F32)
    back = lax.dot_general(
        place,
        jnp.concatenate([sum_out, sum_back], axis=1),
        (((0,), (0,)), ((), ())),
        precision=lax.Precision.HIGHEST,
        preferred_element_type=F32,
    ).astype(BF)
    layer_out = from_relative(back[:, :D], z, h)
    grad_tokens = from_relative(back[:, D:], z, h)
    return (layer_out, grad_tokens, grad_gate)


def solution(mesh):
    fine = Mesh(mesh.devices.reshape(NZ, 2, 4, 4, 2), AXES)
    dp = ("z", "h")
    placed = (
        P(AXES, None),
        P(AXES, None),
        P(AXES, None),
        P(AXES, None),
        P(EP, dp, None),
        P(EP, dp, None),
        P(EP, None, dp),
    )
    return jax.shard_map(
        per_device,
        mesh=fine,
        in_specs=placed,
        out_specs=(P(AXES, None), P(AXES, None), P(EP, dp, None)),
        check_vma=False,
    )
```

time: 591 us -> 291 us (0.49)
  the two profiles are of different devices: /device:TPU:8 before, /device:TPU:2 now
where the time goes in v1:
time: 291 us; the launch traced here: 290 us
  starting transfers between devices  134 us (46%)
  waiting for transfers between devices  112 us (38%)
  Pallas kernels  20.7 us (7%)
  local copies, waits for them, and re-layouts  12.2 us (4%)
  other arithmetic  7.68 us (3%)
    ppermute x14, starting transfers between devices, left(): return lax.ppermute(v, 'z', LEFT)  74.6 us
    ppermute x1, waiting for transfers between devices, per_device(): b[0] = lax.ppermute(own, 'h', SWAP)  58 us
    ppermute x14, waiting for transfers between devices, left(): return lax.ppermute(v, 'z', LEFT)  34.7 us
    ppermute x14, starting transfers between devices, right(): return lax.ppermute(v, 'z', RIGHT)  33.4 us
    all_to_all x2, starting transfers between devices, per_device(): got = lax.all_to_all(payload, EP, 0, 0, tiled=True)  17.6 us
    pallas_call x1, Pallas kernels, hidden_call(): pl.pallas_call(hidden_kernel, out_shape=[jax.ShapeDtypeStruct((ROWS, HID)...  11.3 us
    ppermute x14, waiting for transfers between devices, right(): return lax.ppermute(v, 'z', RIGHT)  9.89 us
    ppermute x1, waiting for transfers between devices, per_device(): crossed = lax.ppermute(other_sum, 'h', SWAP)  9.83 us
  transfers between devices with their start and end apart: 32, of which 14 were waited for; matrix products, arithmetic and copies ran while one was open for 2% of the time, Pallas kernels for 0%

profile of v1, /device:TPU:2, one launch (start us, length us, event | category | flops | bytes accessed | tf_op | source)
XLA Modules:
  0.0 289.7 jit_solution(2797499157746412196)
XLA Ops:
  8.4 9.8 %all-to-all-start = ((bf16[32,18,8,256]{3,2,1,0:T(8,128)(2,1)}), bf16[32,18,8,256]{3,2,1,0:T(8,128)(2,1)S(1)}, u32[]{:S(2)}, u32[]{:S(2)}) async-start(bf16[32,18,8,256]{3,2,1,0:T(8,128)(2,1)} %bitcast.59), calls=%async_computation | async-start | bytes 4718592 | tf_op jit(solution)/shard_map/all_to_all | solution.py:168
  21.9 4.3 %collective-permute-start.7 = (bf16[128,2304]{1,0:T(8,128)(2,1)S(1)}, bf16[128,2304]{1,0:T(8,128)(2,1)S(1)}, u32[]{:S(2)}, u32[]{:S(2)}) collective-permute-start(bf16[128,2304]{1,0:T(8,128)(2,1)S(1)} %pad_maximum_fusion.2.refs_0_), channel_id=1, source_target_pairs={{0,64},{64,128},{128,192},{192,256},{256,320},{320,384},{384,448},... | collective-permute-start | bytes 1769480 | tf_op jit(solution)/shard_map/ppermute | solution.py:105
  26.2 58.0 %collective-permute-done.refs_1_ = bf16[128,2304]{1,0:T(8,128)(2,1)S(1)} collective-permute-done((bf16[128,2304]{1,0:T(8,128)(2,1)S(1)}, bf16[128,2304]{1,0:T(8,128)(2,1)S(1)}, u32[]{:S(2)}, u32[]{:S(2)}) %collective-permute-start) | collective-permute-done | bytes 589856 | tf_op jit(solution)/shard_map/ppermute | solution.py:133
  84.2 11.0 %collective-permute-start.2 = (bf16[128,2304]{1,0:T(8,128)(2,1)S(1)}, bf16[128,2304]{1,0:T(8,128)(2,1)S(1)}, u32[]{:S(2)}, u32[]{:S(2)}) collective-permute-start(bf16[128,2304]{1,0:T(8,128)(2,1)S(1)} %collective-permute-done.refs_1_), channel_id=1, source_target_pairs={{0,448},{64,0},{128,64},{192,128},{256,192},{320,256},{384,320},{4... | collective-permute-start | bytes 1769480 | tf_op jit(solution)/shard_map/ppermute | solution.py:109
  103.0 5.9 %collective-permute-done.2.refs_3_ = bf16[128,2304]{1,0:T(8,128)(2,1)S(1)} collective-permute-done((bf16[128,2304]{1,0:T(8,128)(2,1)S(1)}, bf16[128,2304]{1,0:T(8,128)(2,1)S(1)}, u32[]{:S(2)}, u32[]{:S(2)}) %collective-permute-start.2) | collective-permute-done | bytes 589856 | tf_op jit(solution)/shard_map/ppermute | solution.py:109
  108.9 5.6 %collective-permute-start.4 = (bf16[128,2304]{1,0:T(8,128)(2,1)S(1)}, bf16[128,2304]{1,0:T(8,128)(2,1)S(1)}, u32[]{:S(2)}, u32[]{:S(2)}) collective-permute-start(bf16[128,2304]{1,0:T(8,128)(2,1)S(1)} %collective-permute-done.2.refs_3_), channel_id=1, source_target_pairs={{0,448},{64,0},{128,64},{192,128},{256,192},{320,256},{384,320},{4... | collective-permute-start | bytes 1769480 | tf_op jit(solution)/shard_map/ppermute | solution.py:109
  114.5 7.0 %collective-permute-done.1.refs_2_ = bf16[128,2304]{1,0:T(8,128)(2,1)S(1)} collective-permute-done((bf16[128,2304]{1,0:T(8,128)(2,1)S(1)}, bf16[128,2304]{1,0:T(8,128)(2,1)S(1)}, u32[]{:S(2)}, u32[]{:S(2)}) %collective-permute-start.1) | collective-permute-done | bytes 589856 | tf_op jit(solution)/shard_map/ppermute | solution.py:109
  121.5 5.6 %collective-permute-start.3 = (bf16[128,2304]{1,0:T(8,128)(2,1)S(1)}, bf16[128,2304]{1,0:T(8,128)(2,1)}, u32[]{:S(2)}, u32[]{:S(2)}) collective-permute-start(bf16[128,2304]{1,0:T(8,128)(2,1)S(1)} %collective-permute-done.1.refs_2_), channel_id=1, source_target_pairs={{0,448},{64,0},{128,64},{192,128},{256,192},{320,256},{384,320},{4... | collective-permute-start | bytes 1769480 | tf_op jit(solution)/shard_map/ppermute | solution.py:109
  134.2 5.6 %collective-permute-start.6 = (bf16[128,2304]{1,0:T(8,128)(2,1)S(1)}, bf16[128,2304]{1,0:T(8,128)(2,1)}, u32[]{:S(2)}, u32[]{:S(2)}) collective-permute-start(bf16[128,2304]{1,0:T(8,128)(2,1)S(1)} %collective-permute-done.4.refs_5_), channel_id=1, source_target_pairs={{0,448},{64,0},{128,64},{192,128},{256,192},{320,256},{384,320},{4... | collective-permute-start | bytes 1769480 | tf_op jit(solution)/shard_map/ppermute | solution.py:109
  139.8 7.0 %collective-permute-done.3.refs_4_ = bf16[128,2304]{1,0:T(8,128)(2,1)} collective-permute-done((bf16[128,2304]{1,0:T(8,128)(2,1)S(1)}, bf16[128,2304]{1,0:T(8,128)(2,1)}, u32[]{:S(2)}, u32[]{:S(2)}) %collective-permute-start.3) | collective-permute-done | bytes 589856 | tf_op jit(solution)/shard_map/ppermute | solution.py:109
  146.8 5.7 %collective-permute-start.5 = (bf16[128,2304]{1,0:T(8,128)(2,1)}, bf16[128,2304]{1,0:T(8,128)(2,1)}, u32[]{:S(2)}, u32[]{:S(2)}) collective-permute-start(bf16[128,2304]{1,0:T(8,128)(2,1)} %collective-permute-done.3.refs_4_), channel_id=1, source_target_pairs={{0,448},{64,0},{128,64},{192,128},{256,192},{320,256},{384,320},{4... | collective-permute-start | bytes 1769480 | tf_op jit(solution)/shard_map/ppermute | solution.py:109
  159.5 5.9 %collective-permute-start.11 = (bf16[128,2304]{1,0:T(8,128)(2,1)}, bf16[128,2304]{1,0:T(8,128)(2,1)}, u32[]{:S(2)}, u32[]{:S(2)}) collective-permute-start(bf16[128,2304]{1,0:T(8,128)(2,1)} %collective-permute-done.6.refs_7_), channel_id=1, source_target_pairs={{0,448},{64,0},{128,64},{192,128},{256,192},{320,256},{384,320},{4... | collective-permute-start | bytes 1769480 | tf_op jit(solution)/shard_map/ppermute | solution.py:109
  172.2 8.6 %collective-permute-done.14.refs_11_ = bf16[128,2304]{1,0:T(8,128)(2,1)} collective-permute-done((bf16[128,2304]{1,0:T(8,128)(2,1)}, bf16[128,2304]{1,0:T(8,128)(2,1)}, u32[]{:S(2)}, u32[]{:S(2)}) %collective-permute-start.14) | collective-permute-done | bytes 589856 | tf_op jit(solution)/shard_map/ppermute | solution.py:105
  183.4 11.3 %shard_map.94 = (bf16[288,768]{1,0:T(8,128)(2,1)}, bf16[288,1536]{1,0:T(8,128)(2,1)}, bf16[128,768]{1,0:T(8,128)(2,1)}, bf16[128,768]{1,0:T(8,128)(2,1)}, bf16[1...) custom-call(bf16[288,2048]{1,0:T(8,128)(2,1)} %bitcast.70, ...), custom_call_target="tpu_custom_call" | custom-call | flops 3623878656 | bytes 17000000 | tf_op jit(solution)/shard_map/pallas_call | solution.py:76
  194.7 9.5 %shard_map.95 = (bf16[288,2048]{1,0:T(8,128)(2,1)}, bf16[288,2048]{1,0:T(8,128)(2,1)}) custom-call(bf16[288,768]{1,0:T(8,128)(2,1)} %get-tuple-element.23.h_ref, bf16[288,1536]{1,0:T(8,128)(2,1)} %get-tuple-element.24.d_ref, bf16[128,2304]{1,0:T(8,128)(2,1)} %copy-done, bf16[128,2304]{1,0:T(8,128)(2,1)} %copy-done.2, bf16[128,2304]{1,0:T(8,128)(2,1)} %copy-done.5, ...), custom_call_target="tpu_custom_call" | custom-call | flops 2717908992 | bytes 14000000 | tf_op jit(solution)/shard_map/pallas_call | solution.py:93
  207.9 7.9 %all-to-all-start.1 = ((bf16[32,18,8,256]{3,2,1,0:T(8,128)(2,1)}), bf16[32,18,8,256]{3,2,1,0:T(8,128)(2,1)S(1)}, u32[]{:S(2)}, u32[]{:S(2)}) async-start(bf16[32,18,8,256]{3,2,1,0:T(8,128)(2,1)} %pad_maximum_fusion), calls=%async_computation.1 | async-start | bytes 4718592 | tf_op jit(solution)/shard_map/all_to_all | solution.py:198
  217.9 5.6 %collective-permute-start.19 = (bf16[128,768]{1,0:T(8,128)(2,1)S(1)}, bf16[128,768]{1,0:T(8,128)(2,1)S(1)}, u32[]{:S(2)}, u32[]{:S(2)}) collective-permute-start(bf16[128,768]{1,0:T(8,128)(2,1)S(1)} %copy-done.27), channel_id=1, source_target_pairs={{0,448},{64,0},{128,64},{192,128},{256,192},{320,256},{384,320},{4... | collective-permute-start | bytes 589832 | tf_op jit(solution)/shard_map/ppermute | solution.py:109
  225.4 5.1 %collective-permute-start.25 = (bf16[128,768]{1,0:T(8,128)(2,1)S(1)}, bf16[128,768]{1,0:T(8,128)(2,1)S(1)}, u32[]{:S(2)}, u32[]{:S(2)}) collective-permute-start(bf16[128,768]{1,0:T(8,128)(2,1)S(1)} %copy-done.25), channel_id=1, source_target_pairs={{0,448},{64,0},{128,64},{192,128},{256,192},{320,256},{384,320},{4... | collective-permute-start | bytes 589832 | tf_op jit(solution)/shard_map/ppermute | solution.py:109
  232.8 5.3 %collective-permute-start.20 = (bf16[128,768]{1,0:T(8,128)(2,1)S(1)}, bf16[128,768]{1,0:T(8,128)(2,1)S(1)}, u32[]{:S(2)}, u32[]{:S(2)}) collective-permute-start(bf16[128,768]{1,0:T(8,128)(2,1)S(1)} %add_convert_fusion.8), channel_id=1, source_target_pairs={{0,448},{64,0},{128,64},{192,128},{256,192},{320,256},{384,320},{4... | collective-permute-start | bytes 589832 | tf_op jit(solution)/shard_map/ppermute | solution.py:109
  240.3 5.3 %collective-permute-start.26 = (bf16[128,768]{1,0:T(8,128)(2,1)S(1)}, bf16[128,768]{1,0:T(8,128)(2,1)S(1)}, u32[]{:S(2)}, u32[]{:S(2)}) collective-permute-start(bf16[128,768]{1,0:T(8,128)(2,1)S(1)} %add_convert_fusion.4), channel_id=1, source_target_pairs={{0,448},{64,0},{128,64},{192,128},{256,192},{320,256},{384,320},{4... | collective-permute-start | bytes 589832 | tf_op jit(solution)/shard_map/ppermute | solution.py:109
  247.8 5.3 %collective-permute-start.21 = (bf16[128,768]{1,0:T(8,128)(2,1)S(1)}, bf16[128,768]{1,0:T(8,128)(2,1)S(1)}, u32[]{:S(2)}, u32[]{:S(2)}) collective-permute-start(bf16[128,768]{1,0:T(8,128)(2,1)S(1)} %add_convert_fusion.7), channel_id=1, source_target_pairs={{0,448},{64,0},{128,64},{192,128},{256,192},{320,256},{384,320},{4... | collective-permute-start | bytes 589832 | tf_op jit(solution)/shard_map/ppermute | solution.py:109
  261.0 4.3 %collective-permute-start.28 = (bf16[128,768]{1,0:T(8,128)(2,1)S(1)}, bf16[128,768]{1,0:T(8,128)(2,1)S(1)}, u32[]{:S(2)}, u32[]{:S(2)}) collective-permute-start(bf16[128,768]{1,0:T(8,128)(2,1)S(1)} %add_convert_fusion.2), channel_id=1, source_target_pairs={{0,448},{64,0},{128,64},{192,128},{256,192},{320,256},{384,320},{4... | collective-permute-start | bytes 589832 | tf_op jit(solution)/shard_map/ppermute | solution.py:109
  268.6 4.9 %collective-permute-start.29 = (bf16[128,768]{1,0:T(8,128)(2,1)S(1)}, bf16[128,768]{1,0:T(8,128)(2,1)}, u32[]{:S(2)}, u32[]{:S(2)}) collective-permute-start(bf16[128,768]{1,0:T(8,128)(2,1)S(1)} %add_convert_fusion.1), channel_id=1, source_target_pairs={{0,32},{32,0},{1,33},{33,1},{2,34},{34,2},{3,35},{35,3},{4,36},{36... | collective-permute-start | bytes 589832 | tf_op jit(solution)/shard_map/ppermute | solution.py:185
  274.1 9.8 %collective-permute-done.29 = bf16[128,768]{1,0:T(8,128)(2,1)} collective-permute-done((bf16[128,768]{1,0:T(8,128)(2,1)S(1)}, bf16[128,768]{1,0:T(8,128)(2,1)}, u32[]{:S(2)}, u32[]{:S(2)}) %collective-permute-start.29) | collective-permute-done | bytes 196640 | tf_op jit(solution)/shard_map/ppermute | solution.py:185
  (158 shorter events, 73.9 us)
Async XLA Ops:
  8.4 157.0 %all-to-all-start = ((bf16[32,18,8,256]{3,2,1,0:T(8,128)(2,1)}), bf16[32,18,8,256]{3,2,1,0:T(8,128)(2,1)S(1)}, u32[]{:S(2)}, u32[]{:S(2)}) async-start(bf16[32,18,8,256]{3,2,1,0:T(8,128)(2,1)} %bitcast.59), calls=%async_computation | async-start | bytes 4718592 | tf_op jit(solution)/shard_map/all_to_all | solution.py:168
  18.4 65.7 %collective-permute-start = (bf16[128,2304]{1,0:T(8,128)(2,1)S(1)}, bf16[128,2304]{1,0:T(8,128)(2,1)S(1)}, u32[]{:S(2)}, u32[]{:S(2)}) collective-permute-start(bf16[128,2304]{1,0:T(8,128)(2,1)S(1)} %pad_maximum_fusion.2.refs_0_), channel_id=1, source_target_pairs={{0,32},{32,0},{1,33},{33,1},{2,34},{34,2},{3,35},{35,3},{4,36},{36... | collective-permute-start | bytes 1769480 | tf_op jit(solution)/shard_map/ppermute | solution.py:133
  21.9 75.7 %collective-permute-start.7 = (bf16[128,2304]{1,0:T(8,128)(2,1)S(1)}, bf16[128,2304]{1,0:T(8,128)(2,1)S(1)}, u32[]{:S(2)}, u32[]{:S(2)}) collective-permute-start(bf16[128,2304]{1,0:T(8,128)(2,1)S(1)} %pad_maximum_fusion.2.refs_0_), channel_id=1, source_target_pairs={{0,64},{64,128},{128,192},{192,256},{256,320},{320,384},{384,448},... | collective-permute-start | bytes 1769480 | tf_op jit(solution)/shard_map/ppermute | solution.py:105
  84.2 24.7 %collective-permute-start.2 = (bf16[128,2304]{1,0:T(8,128)(2,1)S(1)}, bf16[128,2304]{1,0:T(8,128)(2,1)S(1)}, u32[]{:S(2)}, u32[]{:S(2)}) collective-permute-start(bf16[128,2304]{1,0:T(8,128)(2,1)S(1)} %collective-permute-done.refs_1_), channel_id=1, source_target_pairs={{0,448},{64,0},{128,64},{192,128},{256,192},{320,256},{384,320},{4... | collective-permute-start | bytes 1769480 | tf_op jit(solution)/shard_map/ppermute | solution.py:109
  95.2 26.4 %collective-permute-start.1 = (bf16[128,2304]{1,0:T(8,128)(2,1)S(1)}, bf16[128,2304]{1,0:T(8,128)(2,1)S(1)}, u32[]{:S(2)}, u32[]{:S(2)}) collective-permute-start(bf16[128,2304]{1,0:T(8,128)(2,1)S(1)} %pad_maximum_fusion.2.refs_0_), channel_id=1, source_target_pairs={{0,448},{64,0},{128,64},{192,128},{256,192},{320,256},{384,320},{4... | collective-permute-start | bytes 1769480 | tf_op jit(solution)/shard_map/ppermute | solution.py:109
  97.6 29.5 %collective-permute-start.8 = (bf16[128,2304]{1,0:T(8,128)(2,1)S(1)}, bf16[128,2304]{1,0:T(8,128)(2,1)S(1)}, u32[]{:S(2)}, u32[]{:S(2)}) collective-permute-start(bf16[128,2304]{1,0:T(8,128)(2,1)S(1)} %collective-permute-done.7.refs_14_), channel_id=1, source_target_pairs={{0,64},{64,128},{128,192},{192,256},{256,320},{320,384},{384,448},... | collective-permute-start | bytes 1769480 | tf_op jit(solution)/shard_map/ppermute | solution.py:105
  101.0 28.1 %collective-permute-start.12 = (bf16[128,2304]{1,0:T(8,128)(2,1)S(1)}, bf16[128,2304]{1,0:T(8,128)(2,1)S(1)}, u32[]{:S(2)}, u32[]{:S(2)}) collective-permute-start(bf16[128,2304]{1,0:T(8,128)(2,1)S(1)} %collective-permute-done.refs_1_), channel_id=1, source_target_pairs={{0,64},{64,128},{128,192},{192,256},{256,320},{320,384},{384,448},... | collective-permute-start | bytes 1769480 | tf_op jit(solution)/shard_map/ppermute | solution.py:105
  108.9 25.3 %collective-permute-start.4 = (bf16[128,2304]{1,0:T(8,128)(2,1)S(1)}, bf16[128,2304]{1,0:T(8,128)(2,1)S(1)}, u32[]{:S(2)}, u32[]{:S(2)}) collective-permute-start(bf16[128,2304]{1,0:T(8,128)(2,1)S(1)} %collective-permute-done.2.refs_3_), channel_id=1, source_target_pairs={{0,448},{64,0},{128,64},{192,128},{256,192},{320,256},{384,320},{4... | collective-permute-start | bytes 1769480 | tf_op jit(solution)/shard_map/ppermute | solution.py:109
  121.5 25.3 %collective-permute-start.3 = (bf16[128,2304]{1,0:T(8,128)(2,1)S(1)}, bf16[128,2304]{1,0:T(8,128)(2,1)}, u32[]{:S(2)}, u32[]{:S(2)}) collective-permute-start(bf16[128,2304]{1,0:T(8,128)(2,1)S(1)} %collective-permute-done.1.refs_2_), channel_id=1, source_target_pairs={{0,448},{64,0},{128,64},{192,128},{256,192},{320,256},{384,320},{4... | collective-permute-start | bytes 1769480 | tf_op jit(solution)/shard_map/ppermute | solution.py:109
  127.2 25.4 %collective-permute-start.9 = (bf16[128,2304]{1,0:T(8,128)(2,1)S(1)}, bf16[128,2304]{1,0:T(8,128)(2,1)}, u32[]{:S(2)}, u32[]{:S(2)}) collective-permute-start(bf16[128,2304]{1,0:T(8,128)(2,1)S(1)} %collective-permute-done.8.refs_12_), channel_id=1, source_target_pairs={{0,64},{64,128},{128,192},{192,256},{256,320},{320,384},{384,448},... | collective-permute-start | bytes 1769480 | tf_op jit(solution)/shard_map/ppermute | solution.py:105
  129.1 26.1 %collective-permute-start.13 = (bf16[128,2304]{1,0:T(8,128)(2,1)S(1)}, bf16[128,2304]{1,0:T(8,128)(2,1)}, u32[]{:S(2)}, u32[]{:S(2)}) collective-permute-start(bf16[128,2304]{1,0:T(8,128)(2,1)S(1)} %collective-permute-done.12.refs_15_), channel_id=1, source_target_pairs={{0,64},{64,128},{128,192},{192,256},{256,320},{320,384},{384,448},... | collective-permute-start | bytes 1769480 | tf_op jit(solution)/shard_map/ppermute | solution.py:105
  134.2 25.3 %collective-permute-start.6 = (bf16[128,2304]{1,0:T(8,128)(2,1)S(1)}, bf16[128,2304]{1,0:T(8,128)(2,1)}, u32[]{:S(2)}, u32[]{:S(2)}) collective-permute-start(bf16[128,2304]{1,0:T(8,128)(2,1)S(1)} %collective-permute-done.4.refs_5_), channel_id=1, source_target_pairs={{0,448},{64,0},{128,64},{192,128},{256,192},{320,256},{384,320},{4... | collective-permute-start | bytes 1769480 | tf_op jit(solution)/shard_map/ppermute | solution.py:109
  146.8 25.4 %collective-permute-start.5 = (bf16[128,2304]{1,0:T(8,128)(2,1)}, bf16[128,2304]{1,0:T(8,128)(2,1)}, u32[]{:S(2)}, u32[]{:S(2)}) collective-permute-start(bf16[128,2304]{1,0:T(8,128)(2,1)} %collective-permute-done.3.refs_4_), channel_id=1, source_target_pairs={{0,448},{64,0},{128,64},{192,128},{256,192},{320,256},{384,320},{4... | collective-permute-start | bytes 1769480 | tf_op jit(solution)/shard_map/ppermute | solution.py:109
  152.5 19.7 %collective-permute-start.10 = (bf16[128,2304]{1,0:T(8,128)(2,1)}, bf16[128,2304]{1,0:T(8,128)(2,1)}, u32[]{:S(2)}, u32[]{:S(2)}) collective-permute-start(bf16[128,2304]{1,0:T(8,128)(2,1)} %collective-permute-done.9.refs_10_), channel_id=1, source_target_pairs={{0,64},{64,128},{128,192},{192,256},{256,320},{320,384},{384,448},... | collective-permute-start | bytes 1769480 | tf_op jit(solution)/shard_map/ppermute | solution.py:105
  155.2 25.6 %collective-permute-start.14 = (bf16[128,2304]{1,0:T(8,128)(2,1)}, bf16[128,2304]{1,0:T(8,128)(2,1)}, u32[]{:S(2)}, u32[]{:S(2)}) collective-permute-start(bf16[128,2304]{1,0:T(8,128)(2,1)} %collective-permute-done.13.refs_13_), channel_id=1, source_target_pairs={{0,64},{64,128},{128,192},{192,256},{256,320},{320,384},{384,448},... | collective-permute-start | bytes 1769480 | tf_op jit(solution)/shard_map/ppermute | solution.py:105
  159.5 23.9 %collective-permute-start.11 = (bf16[128,2304]{1,0:T(8,128)(2,1)}, bf16[128,2304]{1,0:T(8,128)(2,1)}, u32[]{:S(2)}, u32[]{:S(2)}) collective-permute-start(bf16[128,2304]{1,0:T(8,128)(2,1)} %collective-permute-done.6.refs_7_), channel_id=1, source_target_pairs={{0,448},{64,0},{128,64},{192,128},{256,192},{320,256},{384,320},{4... | collective-permute-start | bytes 1769480 | tf_op jit(solution)/shard_map/ppermute | solution.py:109
  207.9 77.8 %all-to-all-start.1 = ((bf16[32,18,8,256]{3,2,1,0:T(8,128)(2,1)}), bf16[32,18,8,256]{3,2,1,0:T(8,128)(2,1)S(1)}, u32[]{:S(2)}, u32[]{:S(2)}) async-start(bf16[32,18,8,256]{3,2,1,0:T(8,128)(2,1)} %pad_maximum_fusion), calls=%async_computation.1 | async-start | bytes 4718592 | tf_op jit(solution)/shard_map/all_to_all | solution.py:198
  217.9 14.9 %collective-permute-start.19 = (bf16[128,768]{1,0:T(8,128)(2,1)S(1)}, bf16[128,768]{1,0:T(8,128)(2,1)S(1)}, u32[]{:S(2)}, u32[]{:S(2)}) collective-permute-start(bf16[128,768]{1,0:T(8,128)(2,1)S(1)} %copy-done.27), channel_id=1, source_target_pairs={{0,448},{64,0},{128,64},{192,128},{256,192},{320,256},{384,320},{4... | collective-permute-start | bytes 589832 | tf_op jit(solution)/shard_map/ppermute | solution.py:109
  230.7 14.9 %collective-permute-start.16 = (bf16[128,768]{1,0:T(8,128)(2,1)S(1)}, bf16[128,768]{1,0:T(8,128)(2,1)S(1)}, u32[]{:S(2)}, u32[]{:S(2)}) collective-permute-start(bf16[128,768]{1,0:T(8,128)(2,1)S(1)} %add_convert_fusion.11), channel_id=1, source_target_pairs={{0,64},{64,128},{128,192},{192,256},{256,320},{320,384},{384,448},... | collective-permute-start | bytes 589832 | tf_op jit(solution)/shard_map/ppermute | solution.py:105
  232.8 14.9 %collective-permute-start.20 = (bf16[128,768]{1,0:T(8,128)(2,1)S(1)}, bf16[128,768]{1,0:T(8,128)(2,1)S(1)}, u32[]{:S(2)}, u32[]{:S(2)}) collective-permute-start(bf16[128,768]{1,0:T(8,128)(2,1)S(1)} %add_convert_fusion.8), channel_id=1, source_target_pairs={{0,448},{64,0},{128,64},{192,128},{256,192},{320,256},{384,320},{4... | collective-permute-start | bytes 589832 | tf_op jit(solution)/shard_map/ppermute | solution.py:109
  238.2 17.1 %collective-permute-start.23 = (bf16[128,768]{1,0:T(8,128)(2,1)S(1)}, bf16[128,768]{1,0:T(8,128)(2,1)S(1)}, u32[]{:S(2)}, u32[]{:S(2)}) collective-permute-start(bf16[128,768]{1,0:T(8,128)(2,1)S(1)} %add_convert_fusion.6), channel_id=1, source_target_pairs={{0,64},{64,128},{128,192},{192,256},{256,320},{320,384},{384,448},... | collective-permute-start | bytes 589832 | tf_op jit(solution)/shard_map/ppermute | solution.py:105
  245.7 19.6 %collective-permute-start.17 = (bf16[128,768]{1,0:T(8,128)(2,1)S(1)}, bf16[128,768]{1,0:T(8,128)(2,1)S(1)}, u32[]{:S(2)}, u32[]{:S(2)}) collective-permute-start(bf16[128,768]{1,0:T(8,128)(2,1)S(1)} %add_convert_fusion.10), channel_id=1, source_target_pairs={{0,64},{64,128},{128,192},{192,256},{256,320},{320,384},{384,448},... | collective-permute-start | bytes 589832 | tf_op jit(solution)/shard_map/ppermute | solution.py:105
  247.8 25.7 %collective-permute-start.21 = (bf16[128,768]{1,0:T(8,128)(2,1)S(1)}, bf16[128,768]{1,0:T(8,128)(2,1)S(1)}, u32[]{:S(2)}, u32[]{:S(2)}) collective-permute-start(bf16[128,768]{1,0:T(8,128)(2,1)S(1)} %add_convert_fusion.7), channel_id=1, source_target_pairs={{0,448},{64,0},{128,64},{192,128},{256,192},{320,256},{384,320},{4... | collective-permute-start | bytes 589832 | tf_op jit(solution)/shard_map/ppermute | solution.py:109
  268.6 15.3 %collective-permute-start.29 = (bf16[128,768]{1,0:T(8,128)(2,1)S(1)}, bf16[128,768]{1,0:T(8,128)(2,1)}, u32[]{:S(2)}, u32[]{:S(2)}) collective-permute-start(bf16[128,768]{1,0:T(8,128)(2,1)S(1)} %add_convert_fusion.1), channel_id=1, source_target_pairs={{0,32},{32,0},{1,33},{33,1},{2,34},{34,2},{3,35},{35,3},{4,36},{36... | collective-permute-start | bytes 589832 | tf_op jit(solution)/shard_map/ppermute | solution.py:185
  (37 other events, 876.3 us)

commit v2 on v1

v2 whole, which is shorter than its diff:
```python
import jax
import jax.numpy as jnp
from jax import lax
from jax.experimental import pallas as pl
from jax.experimental.pallas import tpu as pltpu
from jax.sharding import Mesh, PartitionSpec as P

EXPERTS = 8
CAP = 9
NZ = 8
AXES = ("z", "h", "y", "e", "l", "c")
EP = ("y", "e", "l", "c")
GROUP = ("y", "e")
RIGHT = [(i, (i + 1) % NZ) for i in range(NZ)]
LEFT = [(i, (i - 1) % NZ) for i in range(NZ)]
SWAP = [(0, 1), (1, 0)]
BF = jnp.bfloat16
F32 = jnp.float32
VMEM_LIMIT = 8 * 1024 * 1024
ORDER = (0, 1, 7, 2, 6, 3, 5, 4)
PLACE = tuple(ORDER.index(k) for k in range(NZ))
ROWS = 288
D = 2048
HID = 768


HALF = D // 2
PARTIAL_FLOPS = 30_000_000_000


def pair(pieces, p, at, width):
    return jnp.concatenate([pieces[2 * p][:, at : at + width], pieces[2 * p + 1][:, at : at + width]], axis=0)


def half_dot(v_ref, start, pieces, at):
    acc = None
    for p in range(NZ // 2):
        left = start + p * 256
        term = jnp.dot(v_ref[:, left : left + 256], pair(pieces, p, at, 256), preferred_element_type=F32)
        acc = term if acc is None else acc + term
    return acc


def partial_kernel(x_ref, y_ref, *refs):
    pieces, acc_ref = refs[:NZ], refs[NZ]
    for m in range(3 * HID // 256):
        at = m * 256
        acc_ref[:, at : at + 256] = half_dot(x_ref if m < 6 else y_ref, 0, pieces, at)


def hidden_kernel(x_ref, y_ref, acc_ref, *refs):
    pieces = refs[:16]
    keep_ref, send_ref, d_ref, h_ref = refs[16:]

    def pre(v_ref, at):
        return acc_ref[:, at : at + 256] + half_dot(v_ref, HALF, pieces[NZ:], at)

    for m in range(HID // 256):
        at = m * 256
        g = pre(x_ref, at)
        u = pre(x_ref, HID + at)
        dh = pre(y_ref, 2 * HID + at)
        s = 1.0 / (1.0 + jnp.exp(-g))
        gs = g * s
        h_ref[:, at : at + 256] = (gs * u).astype(BF)
        d_ref[:, HID + at : HID + at + 256] = (dh * gs).astype(BF)
        d_ref[:, at : at + 256] = (dh * u * s * (1.0 + g * (1.0 - s))).astype(BF)
    last = (((1,), (1,)), ((), ()))
    half = ROWS // 2
    for p in range(NZ):
        at = p * 256
        out = lax.dot_general(h_ref[...], pair(pieces, p, 2 * HID, HID), last, preferred_element_type=F32)
        back = lax.dot_general(d_ref[...], pair(pieces, p, 0, 2 * HID), last, preferred_element_type=F32)
        for j, v in enumerate((out, back)):
            keep_ref[j, :, at : at + 256] = v[:half].astype(BF)
            send_ref[j, :, at : at + 256] = v[half:].astype(BF)


def gate_kernel(x_ref, d_ref, *gg):
    dg = d_ref[:, :HID]
    for p in range(NZ):
        for g in range(2):
            at = g * HALF + p * 128
            gg[p][g * 128 : (g + 1) * 128, :] = lax.dot_general(
                x_ref[:, at : at + 128], dg, (((0,), (0,)), ((), ())), preferred_element_type=F32
            ).astype(BF)


VM = pl.BlockSpec(memory_space=pltpu.VMEM)


def params():
    return pltpu.CompilerParams(vmem_limit_bytes=VMEM_LIMIT)


def cost(flops, size):
    return pl.CostEstimate(flops=flops, bytes_accessed=size, transcendentals=0)


def partial_call(x, y, pieces):
    return pl.pallas_call(
        partial_kernel,
        out_shape=jax.ShapeDtypeStruct((ROWS, 3 * HID), F32),
        in_specs=[VM] * (2 + NZ),
        out_specs=VM,
        compiler_params=params(),
        cost_estimate=cost(PARTIAL_FLOPS, 10_000_000),
    )(x, y, *pieces)


def hidden_call(x, y, acc, pieces):
    return pl.pallas_call(
        hidden_kernel,
        out_shape=[jax.ShapeDtypeStruct((2, ROWS // 2, D), BF)] * 2 + [jax.ShapeDtypeStruct((ROWS, 2 * HID), BF)],
        in_specs=[VM] * 19,
        out_specs=[VM] * 3,
        scratch_shapes=[pltpu.VMEM((ROWS, HID), BF)],
        compiler_params=params(),
        cost_estimate=cost(2 * ROWS * D * HID * 3, 20_000_000),
    )(x, y, acc, *pieces)


def gate_call(x, d):
    return pl.pallas_call(
        gate_kernel,
        out_shape=[jax.ShapeDtypeStruct((256, HID), BF)] * NZ,
        in_specs=[VM] * 2,
        out_specs=[VM] * NZ,
        compiler_params=params(),
        cost_estimate=cost(2 * ROWS * D * HID, 6_000_000),
    )(x, d)


def right(v):
    return lax.ppermute(v, "z", RIGHT)


def left(v):
    return lax.ppermute(v, "z", LEFT)


def add(a, b):
    return (a.astype(F32) + b.astype(F32)).astype(BF)


def to_relative(v, z, h):
    rolled = lax.dynamic_slice(jnp.concatenate([v, v], axis=1), (0, z * 256), v.shape)
    even, odd = (
        jnp.concatenate([rolled[:, k * 256 + g * 128 : k * 256 + g * 128 + 128] for k in ORDER], axis=1)
        for g in range(2)
    )
    return jnp.concatenate([jnp.where(h == 0, even, odd), jnp.where(h == 0, odd, even)], axis=1)


def from_relative(v, z, h):
    even = jnp.where(h == 0, v[:, :HALF], v[:, HALF:])
    odd = jnp.where(h == 0, v[:, HALF:], v[:, :HALF])
    parts = jnp.concatenate([t[:, p * 128 : p * 128 + 128] for p in PLACE for t in (even, odd)], axis=1)
    return lax.dynamic_slice(jnp.concatenate([parts, parts], axis=1), (0, (NZ - z) * 256), v.shape)


def per_device(tokens, grad_out, expert_ids, combine, w_gate, w_up, w_down):
    z, h = lax.axis_index("z"), lax.axis_index("h")
    own = jnp.concatenate([w_gate[0], w_up[0], w_down[0].T], axis=1)
    a, b = [None] * NZ, [None] * NZ
    b[0] = lax.ppermute(own, "h", SWAP)
    both = jnp.concatenate([to_relative(tokens, z, h), to_relative(grad_out, z, h)], axis=1)
    e0, e1 = expert_ids[:, 0], expert_ids[:, 1]
    before = jnp.arange(32)[None, :] < jnp.arange(32)[:, None]

    def count(mine):
        hit = (e0[None, :] == mine[:, None]).astype(jnp.int32) + (e1[None, :] == mine[:, None]).astype(jnp.int32)
        return jnp.sum(jnp.where(before, hit, 0), axis=1)

    t0, t1 = e0 * CAP + count(e0), e1 * CAP + count(e1)
    slots = jnp.arange(EXPERTS * CAP, dtype=jnp.int32)[:, None]
    hit0, hit1 = slots == t0[None, :], slots == t1[None, :]
    pick = (hit0 | hit1).astype(BF)
    scale = jnp.sum(
        jnp.where(hit0, combine[:, 0][None, :], 0.0) + jnp.where(hit1, combine[:, 1][None, :], 0.0), axis=1
    )
    picked = jnp.dot(pick, both, preferred_element_type=F32)
    a[0] = own
    for s in range(1, 5):
        a[NZ - s] = right(a[(NZ - s + 1) % NZ])
        if s < 4:
            a[s] = left(a[s - 1])
    for s in range(1, 5):
        if s < 4:
            b[NZ - s] = right(b[(NZ - s + 1) % NZ])
        b[s] = left(b[s - 1])
    mine = [a[k] for k in ORDER]
    pieces = mine + [b[k] for k in ORDER]

    routed_x = picked[:, :D].astype(BF)
    routed_y = (picked[:, D:] * scale[:, None]).astype(BF)

    def fold(v, lead):
        return v.reshape(lead, CAP, 8, 256)

    payload = jnp.concatenate([fold(routed_x, EXPERTS), fold(routed_y, EXPERTS)], axis=1)
    block = lax.all_to_all(payload, GROUP, 0, 0, tiled=True)
    beside = lax.ppermute(block, "l", SWAP)
    quarters = (block, beside, lax.ppermute(block, "c", SWAP), lax.ppermute(beside, "c", SWAP))
    x = jnp.concatenate([q[:, :CAP].reshape(ROWS // 4, D) for q in quarters], axis=0)
    y = jnp.concatenate([q[:, CAP:].reshape(ROWS // 4, D) for q in quarters], axis=0)

    acc = partial_call(x, y, mine)
    keep, send, dgu = hidden_call(x, y, acc, pieces)
    gg = gate_call(x, dgu)
    crossed = lax.ppermute(send, "c", SWAP)
    quarter = (keep.astype(F32) + crossed.astype(F32)).astype(BF).reshape(2, 2, 72, D)
    summed = add(quarter[:, 0], lax.ppermute(quarter[:, 1], "l", SWAP))
    payload = jnp.concatenate([fold(summed[0], EXPERTS), fold(summed[1], EXPERTS)], axis=1)
    got = lax.all_to_all(payload, GROUP, 0, 0, tiled=True)

    gg = [gg[p] for p in PLACE]
    r, l = gg[4], gg[5]
    for s in range(1, 5):
        r = right(r)
        if s < 4:
            r = add(r, gg[4 - s])
            l = left(l)
            if s < 3:
                l = add(l, gg[5 + s])
    near = r.astype(F32) + l.astype(F32) + gg[0].astype(F32)
    crossed = lax.ppermute(near[128:].astype(BF), "h", SWAP)
    grad_gate = (near[:128] + crossed.astype(F32)).astype(BF)[None]

    total = got.astype(F32)
    sum_out = total[:, :CAP].reshape(EXPERTS * CAP, D) * scale[:, None]
    sum_back = total[:, CAP:].reshape(EXPERTS * CAP, D)
    place = (hit0 | hit1).astype(F32)
    back = lax.dot_general(
        place,
        jnp.concatenate([sum_out, sum_back], axis=1),
        (((0,), (0,)), ((), ())),
        precision=lax.Precision.HIGHEST,
        preferred_element_type=F32,
    ).astype(BF)
    layer_out = from_relative(back[:, :D], z, h)
    grad_tokens = from_relative(back[:, D:], z, h)
    return (layer_out, grad_tokens, grad_gate)


def solution(mesh):
    fine = Mesh(mesh.devices.reshape(NZ, 2, 4, 2, 2, 2), AXES)
    dp = ("z", "h")
    placed = (
        P(AXES, None),
        P(AXES, None),
        P(AXES, None),
        P(AXES, None),
        P(EP, dp, None),
        P(EP, dp, None),
        P(EP, None, dp),
    )
    return jax.shard_map(
        per_device,
        mesh=fine,
        in_specs=placed,
        out_specs=(P(AXES, None), P(AXES, None), P(EP, dp, None)),
        check_vma=False,
    )
```

time: 291 us -> 231 us (0.79)
  the two profiles are of different devices: /device:TPU:2 before, /device:TPU:8 now
where the time goes in v2:
time: 231 us; the launch traced here: 229 us
  starting transfers between devices  130 us (56%)
  waiting for transfers between devices  73 us (32%)
  Pallas kernels  10.3 us (4%)
  other arithmetic  6.99 us (3%)
  local copies, waits for them, and re-layouts  6.65 us (3%)
    ppermute x10, starting transfers between devices, left(): return lax.ppermute(v, 'z', LEFT)  57.5 us
    ppermute x10, waiting for transfers between devices, left(): return lax.ppermute(v, 'z', LEFT)  27.5 us
    ppermute x11, starting transfers between devices, right(): return lax.ppermute(v, 'z', RIGHT)  24.6 us
    all_to_all x1, starting transfers between devices, per_device(): got = lax.all_to_all(payload, GROUP, 0, 0, tiled=True)  19.2 us
    ppermute x11, waiting for transfers between devices, right(): return lax.ppermute(v, 'z', RIGHT)  17.8 us
    ppermute x1, waiting for transfers between devices, per_device(): crossed = lax.ppermute(near[128:].astype(BF), 'h', SWAP)  11.6 us
    all_to_all x1, starting transfers between devices, per_device(): block = lax.all_to_all(payload, GROUP, 0, 0, tiled=True)  9.89 us
    ppermute x1, waiting for transfers between devices, per_device(): b[0] = lax.ppermute(own, 'h', SWAP)  6.78 us
  transfers between devices with their start and end apart: 30, of which 14 were waited for; matrix products, arithmetic and copies ran while one was open for 2% of the time, Pallas kernels for 1%

profile of v2, /device:TPU:8, one launch (start us, length us, event | category | flops | bytes accessed | tf_op | source)
XLA Modules:
  0.0 229.4 jit_solution(5121235621643494068)
XLA Ops:
  7.1 9.9 %all-to-all-start = ((bf16[8,18,8,256]{3,2,1,0:T(8,128)(2,1)}), bf16[8,18,8,256]{3,2,1,0:T(8,128)(2,1)}, u32[]{:S(2)}, u32[]{:S(2)}) async-start(bf16[8,18,8,256]{3,2,1,0:T(8,128)(2,1)} %pad_maximum_fusion), calls=%async_computation | async-start | bytes 1179648 | tf_op jit(solution)/shard_map/all_to_all | solution.py:202
  20.2 4.3 %collective-permute-start.4 = (bf16[128,2304]{1,0:T(8,128)(2,1)S(1)}, bf16[128,2304]{1,0:T(8,128)(2,1)S(1)}, u32[]{:S(2)}, u32[]{:S(2)}) collective-permute-start(bf16[128,2304]{1,0:T(8,128)(2,1)S(1)} %pad_maximum_fusion.1.refs_0_), channel_id=1, source_target_pairs={{0,64},{64,128},{128,192},{192,256},{256,320},{320,384},{384,448},... | collective-permute-start | bytes 1769480 | tf_op jit(solution)/shard_map/ppermute | solution.py:135
  24.4 8.6 %collective-permute-start.3 = (bf16[128,2304]{1,0:T(8,128)(2,1)S(1)}, bf16[128,2304]{1,0:T(8,128)(2,1)S(1)}, u32[]{:S(2)}, u32[]{:S(2)}) collective-permute-start(bf16[128,2304]{1,0:T(8,128)(2,1)S(1)} %pad_maximum_fusion.1.refs_0_), channel_id=1, source_target_pairs={{0,448},{64,0},{128,64},{192,128},{256,192},{320,256},{384,320},{4... | collective-permute-start | bytes 1769480 | tf_op jit(solution)/shard_map/ppermute | solution.py:139
  33.1 6.8 %collective-permute-done.10.refs_8_ = bf16[128,2304]{1,0:T(8,128)(2,1)S(1)} collective-permute-done((bf16[128,2304]{1,0:T(8,128)(2,1)S(1)}, bf16[128,2304]{1,0:T(8,128)(2,1)S(1)}, u32[]{:S(2)}, u32[]{:S(2)}) %collective-permute-start.10) | collective-permute-done | bytes 589856 | tf_op jit(solution)/shard_map/ppermute | solution.py:166
  42.9 8.6 %collective-permute-start.11 = (bf16[128,2304]{1,0:T(8,128)(2,1)S(1)}, bf16[128,2304]{1,0:T(8,128)(2,1)S(1)}, u32[]{:S(2)}, u32[]{:S(2)}) collective-permute-start(bf16[128,2304]{1,0:T(8,128)(2,1)S(1)} %collective-permute-done.10.refs_8_), channel_id=1, source_target_pairs={{0,448},{64,0},{128,64},{192,128},{256,192},{320,256},{384,320},{4... | collective-permute-start | bytes 1769480 | tf_op jit(solution)/shard_map/ppermute | solution.py:139
  53.5 5.1 %collective-permute-start.5 = (bf16[128,2304]{1,0:T(8,128)(2,1)S(1)}, bf16[128,2304]{1,0:T(8,128)(2,1)}, u32[]{:S(2)}, u32[]{:S(2)}) collective-permute-start(bf16[128,2304]{1,0:T(8,128)(2,1)S(1)} %collective-permute-done.3.refs_1_), channel_id=1, source_target_pairs={{0,448},{64,0},{128,64},{192,128},{256,192},{320,256},{384,320},{4... | collective-permute-start | bytes 1769480 | tf_op jit(solution)/shard_map/ppermute | solution.py:139
  68.7 7.8 %collective-permute-done.6.refs_4_ = bf16[128,2304]{1,0:T(8,128)(2,1)} collective-permute-done((bf16[128,2304]{1,0:T(8,128)(2,1)S(1)}, bf16[128,2304]{1,0:T(8,128)(2,1)}, u32[]{:S(2)}, u32[]{:S(2)}) %collective-permute-start.6) | collective-permute-done | bytes 589856 | tf_op jit(solution)/shard_map/ppermute | solution.py:135
  76.5 3.9 %collective-permute-start.13 = (bf16[128,2304]{1,0:T(8,128)(2,1)S(1)}, bf16[128,2304]{1,0:T(8,128)(2,1)S(1)}, u32[]{:S(2)}, u32[]{:S(2)}) collective-permute-start(bf16[128,2304]{1,0:T(8,128)(2,1)S(1)} %collective-permute-done.11.refs_9_), channel_id=1, source_target_pairs={{0,448},{64,0},{128,64},{192,128},{256,192},{320,256},{384,320},{4... | collective-permute-start | bytes 1769480 | tf_op jit(solution)/shard_map/ppermute | solution.py:139
  82.4 5.1 %collective-permute-start.7 = (bf16[128,2304]{1,0:T(8,128)(2,1)}, bf16[128,2304]{1,0:T(8,128)(2,1)S(1)}, u32[]{:S(2)}, u32[]{:S(2)}) collective-permute-start(bf16[128,2304]{1,0:T(8,128)(2,1)} %collective-permute-done.5.refs_3_), channel_id=1, source_target_pairs={{0,448},{64,0},{128,64},{192,128},{256,192},{320,256},{384,320},{4... | collective-permute-start | bytes 1769480 | tf_op jit(solution)/shard_map/ppermute | solution.py:139
  94.6 5.2 %collective-permute-start.15 = (bf16[128,2304]{1,0:T(8,128)(2,1)S(1)}, bf16[128,2304]{1,0:T(8,128)(2,1)S(1)}, u32[]{:S(2)}, u32[]{:S(2)}) collective-permute-start(bf16[128,2304]{1,0:T(8,128)(2,1)S(1)} %collective-permute-done.13.refs_11_), channel_id=1, source_target_pairs={{0,448},{64,0},{128,64},{192,128},{256,192},{320,256},{384,320},{4... | collective-permute-start | bytes 1769480 | tf_op jit(solution)/shard_map/ppermute | solution.py:139
  103.8 13.5 %collective-permute-done.15.refs_13_ = bf16[128,2304]{1,0:T(8,128)(2,1)S(1)} collective-permute-done((bf16[128,2304]{1,0:T(8,128)(2,1)S(1)}, bf16[128,2304]{1,0:T(8,128)(2,1)S(1)}, u32[]{:S(2)}, u32[]{:S(2)}) %collective-permute-start.15) | collective-permute-done | bytes 589856 | tf_op jit(solution)/shard_map/ppermute | solution.py:139
  117.3 4.5 %collective-permute-start.17 = (bf16[128,2304]{1,0:T(8,128)(2,1)S(1)}, bf16[128,2304]{1,0:T(8,128)(2,1)S(1)}, u32[]{:S(2)}, u32[]{:S(2)}) collective-permute-start(bf16[128,2304]{1,0:T(8,128)(2,1)S(1)} %collective-permute-done.15.refs_13_), channel_id=1, source_target_pairs={{0,448},{64,0},{128,64},{192,128},{256,192},{320,256},{384,320},{4... | collective-permute-start | bytes 1769480 | tf_op jit(solution)/shard_map/ppermute | solution.py:139
  121.8 4.2 %collective-permute-done.9.refs_7_ = bf16[128,2304]{1,0:T(8,128)(2,1)S(1)} collective-permute-done((bf16[128,2304]{1,0:T(8,128)(2,1)S(1)}, bf16[128,2304]{1,0:T(8,128)(2,1)S(1)}, u32[]{:S(2)}, u32[]{:S(2)}) %collective-permute-start.9) | collective-permute-done | bytes 589856 | tf_op jit(solution)/shard_map/ppermute | solution.py:135
  131.9 5.7 %shard_map.95 = (bf16[2,144,2048]{2,1,0:T(8,128)(2,1)S(1)}, bf16[2,144,2048]{2,1,0:T(8,128)(2,1)S(1)}, bf16[288,1536]{1,0:T(8,128)(2,1)S(1)}) custom-call(bf16[288,2048]{1,0:T(8,128)(2,1)S(1)} %constant_dynamic-update-slice_fusion.32.x_ref, bf16[288,2048]{1,0:T(8,128)(2,1)S(1)} %constant_dynamic-update-slice_fusion.36.y_ref, ...), custom_call_target="tpu_custom_call" | custom-call | flops 2717908992 | bytes 20000000 | tf_op jit(solution)/shard_map/pallas_call | solution.py:112
  143.3 5.1 %collective-permute-start.24 = (bf16[256,768]{1,0:T(8,128)(2,1)S(1)}, bf16[256,768]{1,0:T(8,128)(2,1)S(1)}, u32[]{:S(2)}, u32[]{:S(2)}) collective-permute-start(bf16[256,768]{1,0:T(8,128)(2,1)S(1)} %get-tuple-element.21), channel_id=1, source_target_pairs={{0,448},{64,0},{128,64},{192,128},{256,192},{320,256},{384,320},{4... | collective-permute-start | bytes 1179656 | tf_op jit(solution)/shard_map/ppermute | solution.py:139
  152.4 5.1 %collective-permute-done.24 = bf16[256,768]{1,0:T(8,128)(2,1)S(1)} collective-permute-done((bf16[256,768]{1,0:T(8,128)(2,1)S(1)}, bf16[256,768]{1,0:T(8,128)(2,1)S(1)}, u32[]{:S(2)}, u32[]{:S(2)}) %collective-permute-start.24) | collective-permute-done | bytes 393248 | tf_op jit(solution)/shard_map/ppermute | solution.py:139
  157.6 5.6 %collective-permute-start.25 = (bf16[256,768]{1,0:T(8,128)(2,1)S(1)}, bf16[256,768]{1,0:T(8,128)(2,1)S(1)}, u32[]{:S(2)}, u32[]{:S(2)}) collective-permute-start(bf16[256,768]{1,0:T(8,128)(2,1)S(1)} %add_convert_fusion.2), channel_id=1, source_target_pairs={{0,448},{64,0},{128,64},{192,128},{256,192},{320,256},{384,320},{4... | collective-permute-start | bytes 1179656 | tf_op jit(solution)/shard_map/ppermute | solution.py:139
  168.3 3.1 %collective-permute-done.25 = bf16[256,768]{1,0:T(8,128)(2,1)S(1)} collective-permute-done((bf16[256,768]{1,0:T(8,128)(2,1)S(1)}, bf16[256,768]{1,0:T(8,128)(2,1)S(1)}, u32[]{:S(2)}, u32[]{:S(2)}) %collective-permute-start.25) | collective-permute-done | bytes 393248 | tf_op jit(solution)/shard_map/ppermute | solution.py:139
  171.5 5.6 %collective-permute-start.26 = (bf16[256,768]{1,0:T(8,128)(2,1)S(1)}, bf16[256,768]{1,0:T(8,128)(2,1)S(1)}, u32[]{:S(2)}, u32[]{:S(2)}) collective-permute-start(bf16[256,768]{1,0:T(8,128)(2,1)S(1)} %add_convert_fusion.1), channel_id=1, source_target_pairs={{0,448},{64,0},{128,64},{192,128},{256,192},{320,256},{384,320},{4... | collective-permute-start | bytes 1179656 | tf_op jit(solution)/shard_map/ppermute | solution.py:139
  179.1 3.2 %collective-permute-done.19 = bf16[2,72,2048]{2,1,0:T(8,128)(2,1)S(1)} collective-permute-done((bf16[2,72,2048]{2,1,0:T(8,128)(2,1)S(1)}, bf16[2,72,2048]{2,1,0:T(8,128)(2,1)S(1)}, u32[]{:S(2)}, u32[]{:S(2)}) %collective-permute-start.19) | collective-permute-done | bytes 589856 | tf_op jit(solution)/shard_map/ppermute | solution.py:213
  183.5 19.2 %all-to-all-start.1 = ((bf16[8,18,8,256]{3,2,1,0:T(8,128)(2,1)}), bf16[8,18,8,256]{3,2,1,0:T(8,128)(2,1)S(1)}, u32[]{:S(2)}, u32[]{:S(2)}) async-start(bf16[8,18,8,256]{3,2,1,0:T(8,128)(2,1)} %pad_maximum_fusion.2), calls=%async_computation.1 | async-start | bytes 1179648 | tf_op jit(solution)/shard_map/all_to_all | solution.py:215
  202.9 4.6 %collective-permute-start.27 = (bf16[128,768]{1,0:T(8,128)(2,1)S(1)}, bf16[128,768]{1,0:T(8,128)(2,1)S(1)}, u32[]{:S(2)}, u32[]{:S(2)}) collective-permute-start(bf16[128,768]{1,0:T(8,128)(2,1)S(1)} %slice.585), channel_id=1, source_target_pairs={{0,32},{32,0},{1,33},{33,1},{2,34},{34,2},{3,35},{35,3},{4,36},{36... | collective-permute-start | bytes 589832 | tf_op jit(solution)/shard_map/ppermute | solution.py:227
  207.5 11.6 %collective-permute-done.27 = bf16[128,768]{1,0:T(8,128)(2,1)S(1)} collective-permute-done((bf16[128,768]{1,0:T(8,128)(2,1)S(1)}, bf16[128,768]{1,0:T(8,128)(2,1)S(1)}, u32[]{:S(2)}, u32[]{:S(2)}) %collective-permute-start.27) | collective-permute-done | bytes 196640 | tf_op jit(solution)/shard_map/ppermute | solution.py:227
  219.8 6.2 %all-to-all-done.1 = bf16[8,18,8,256]{3,2,1,0:T(8,128)(2,1)S(1)} async-done(((bf16[8,18,8,256]{3,2,1,0:T(8,128)(2,1)}), bf16[8,18,8,256]{3,2,1,0:T(8,128)(2,1)S(1)}, u32[]{:S(2)}, u32[]{:S(2)}) %all-to-all-start.1) | async-done | bytes 589856 | tf_op jit(solution)/shard_map/all_to_all | solution.py:215
  (186 shorter events, 65.3 us)
Async XLA Ops:
  7.1 51.5 %all-to-all-start = ((bf16[8,18,8,256]{3,2,1,0:T(8,128)(2,1)}), bf16[8,18,8,256]{3,2,1,0:T(8,128)(2,1)}, u32[]{:S(2)}, u32[]{:S(2)}) async-start(bf16[8,18,8,256]{3,2,1,0:T(8,128)(2,1)} %pad_maximum_fusion), calls=%async_computation | async-start | bytes 1179648 | tf_op jit(solution)/shard_map/all_to_all | solution.py:202
  17.2 22.6 %collective-permute-start.10 = (bf16[128,2304]{1,0:T(8,128)(2,1)S(1)}, bf16[128,2304]{1,0:T(8,128)(2,1)S(1)}, u32[]{:S(2)}, u32[]{:S(2)}) collective-permute-start(bf16[128,2304]{1,0:T(8,128)(2,1)S(1)} %pad_maximum_fusion.1.refs_0_), channel_id=1, source_target_pairs={{0,32},{32,0},{1,33},{33,1},{2,34},{34,2},{3,35},{35,3},{4,36},{36... | collective-permute-start | bytes 1769480 | tf_op jit(solution)/shard_map/ppermute | solution.py:166
  20.2 31.3 %collective-permute-start.4 = (bf16[128,2304]{1,0:T(8,128)(2,1)S(1)}, bf16[128,2304]{1,0:T(8,128)(2,1)S(1)}, u32[]{:S(2)}, u32[]{:S(2)}) collective-permute-start(bf16[128,2304]{1,0:T(8,128)(2,1)S(1)} %pad_maximum_fusion.1.refs_0_), channel_id=1, source_target_pairs={{0,64},{64,128},{128,192},{192,256},{256,320},{320,384},{384,448},... | collective-permute-start | bytes 1769480 | tf_op jit(solution)/shard_map/ppermute | solution.py:135
  24.4 29.0 %collective-permute-start.3 = (bf16[128,2304]{1,0:T(8,128)(2,1)S(1)}, bf16[128,2304]{1,0:T(8,128)(2,1)S(1)}, u32[]{:S(2)}, u32[]{:S(2)}) collective-permute-start(bf16[128,2304]{1,0:T(8,128)(2,1)S(1)} %pad_maximum_fusion.1.refs_0_), channel_id=1, source_target_pairs={{0,448},{64,0},{128,64},{192,128},{256,192},{320,256},{384,320},{4... | collective-permute-start | bytes 1769480 | tf_op jit(solution)/shard_map/ppermute | solution.py:139
  39.9 23.9 %collective-permute-start.12 = (bf16[128,2304]{1,0:T(8,128)(2,1)S(1)}, bf16[128,2304]{1,0:T(8,128)(2,1)S(1)}, u32[]{:S(2)}, u32[]{:S(2)}) collective-permute-start(bf16[128,2304]{1,0:T(8,128)(2,1)S(1)} %collective-permute-done.10.refs_8_), channel_id=1, source_target_pairs={{0,64},{64,128},{128,192},{192,256},{256,320},{320,384},{384,448},... | collective-permute-start | bytes 1769480 | tf_op jit(solution)/shard_map/ppermute | solution.py:135
  42.9 23.9 %collective-permute-start.11 = (bf16[128,2304]{1,0:T(8,128)(2,1)S(1)}, bf16[128,2304]{1,0:T(8,128)(2,1)S(1)}, u32[]{:S(2)}, u32[]{:S(2)}) collective-permute-start(bf16[128,2304]{1,0:T(8,128)(2,1)S(1)} %collective-permute-done.10.refs_8_), channel_id=1, source_target_pairs={{0,448},{64,0},{128,64},{192,128},{256,192},{320,256},{384,320},{4... | collective-permute-start | bytes 1769480 | tf_op jit(solution)/shard_map/ppermute | solution.py:139
  51.5 24.9 %collective-permute-start.6 = (bf16[128,2304]{1,0:T(8,128)(2,1)S(1)}, bf16[128,2304]{1,0:T(8,128)(2,1)}, u32[]{:S(2)}, u32[]{:S(2)}) collective-permute-start(bf16[128,2304]{1,0:T(8,128)(2,1)S(1)} %collective-permute-done.4.refs_2_), channel_id=1, source_target_pairs={{0,64},{64,128},{128,192},{192,256},{256,320},{320,384},{384,448},... | collective-permute-start | bytes 1769480 | tf_op jit(solution)/shard_map/ppermute | solution.py:135
  53.5 27.0 %collective-permute-start.5 = (bf16[128,2304]{1,0:T(8,128)(2,1)S(1)}, bf16[128,2304]{1,0:T(8,128)(2,1)}, u32[]{:S(2)}, u32[]{:S(2)}) collective-permute-start(bf16[128,2304]{1,0:T(8,128)(2,1)S(1)} %collective-permute-done.3.refs_1_), channel_id=1, source_target_pairs={{0,448},{64,0},{128,64},{192,128},{256,192},{320,256},{384,320},{4... | collective-permute-start | bytes 1769480 | tf_op jit(solution)/shard_map/ppermute | solution.py:139
  58.6 23.8 %collective-permute-start.1 = (bf16[8,18,8,256]{3,2,1,0:T(8,128)(2,1)}, bf16[8,18,8,256]{3,2,1,0:T(8,128)(2,1)S(1)}, u32[]{:S(2)}, u32[]{:S(2)}) collective-permute-start(bf16[8,18,8,256]{3,2,1,0:T(8,128)(2,1)} %all-to-all-done), channel_id=1, source_target_pairs={{0,1},{1,0},{2,3},{3,2},{4,5},{5,4},{6,7},{7,6},{8,9},{9,8},{10,11... | collective-permute-start | bytes 1769480 | tf_op jit(solution)/shard_map/ppermute | solution.py:204
  63.7 24.0 %collective-permute-start = (bf16[8,18,8,256]{3,2,1,0:T(8,128)(2,1)}, bf16[8,18,8,256]{3,2,1,0:T(8,128)(2,1)S(1)}, u32[]{:S(2)}, u32[]{:S(2)}) collective-permute-start(bf16[8,18,8,256]{3,2,1,0:T(8,128)(2,1)} %all-to-all-done), channel_id=1, source_target_pairs={{0,2},{2,0},{1,3},{3,1},{4,6},{6,4},{5,7},{7,5},{8,10},{10,8},{9,1... | collective-permute-start | bytes 1769480 | tf_op jit(solution)/shard_map/ppermute | solution.py:203
  66.7 23.2 %collective-permute-start.14 = (bf16[128,2304]{1,0:T(8,128)(2,1)S(1)}, bf16[128,2304]{1,0:T(8,128)(2,1)S(1)}, u32[]{:S(2)}, u32[]{:S(2)}) collective-permute-start(bf16[128,2304]{1,0:T(8,128)(2,1)S(1)} %collective-permute-done.12.refs_10_), channel_id=1, source_target_pairs={{0,64},{64,128},{128,192},{192,256},{256,320},{320,384},{384,448},... | collective-permute-start | bytes 1769480 | tf_op jit(solution)/shard_map/ppermute | solution.py:135
  76.5 18.1 %collective-permute-start.13 = (bf16[128,2304]{1,0:T(8,128)(2,1)S(1)}, bf16[128,2304]{1,0:T(8,128)(2,1)S(1)}, u32[]{:S(2)}, u32[]{:S(2)}) collective-permute-start(bf16[128,2304]{1,0:T(8,128)(2,1)S(1)} %collective-permute-done.11.refs_9_), channel_id=1, source_target_pairs={{0,448},{64,0},{128,64},{192,128},{256,192},{320,256},{384,320},{4... | collective-permute-start | bytes 1769480 | tf_op jit(solution)/shard_map/ppermute | solution.py:139
  80.4 21.2 %collective-permute-start.8 = (bf16[128,2304]{1,0:T(8,128)(2,1)}, bf16[128,2304]{1,0:T(8,128)(2,1)S(1)}, u32[]{:S(2)}, u32[]{:S(2)}) collective-permute-start(bf16[128,2304]{1,0:T(8,128)(2,1)} %collective-permute-done.6.refs_4_), channel_id=1, source_target_pairs={{0,64},{64,128},{128,192},{192,256},{256,320},{320,384},{384,448},... | collective-permute-start | bytes 1769480 | tf_op jit(solution)/shard_map/ppermute | solution.py:135
  82.4 39.5 %collective-permute-start.7 = (bf16[128,2304]{1,0:T(8,128)(2,1)}, bf16[128,2304]{1,0:T(8,128)(2,1)S(1)}, u32[]{:S(2)}, u32[]{:S(2)}) collective-permute-start(bf16[128,2304]{1,0:T(8,128)(2,1)} %collective-permute-done.5.refs_3_), channel_id=1, source_target_pairs={{0,448},{64,0},{128,64},{192,128},{256,192},{320,256},{384,320},{4... | collective-permute-start | bytes 1769480 | tf_op jit(solution)/shard_map/ppermute | solution.py:139
  87.9 15.6 %collective-permute-start.2 = (bf16[8,18,8,256]{3,2,1,0:T(8,128)(2,1)S(1)}, bf16[8,18,8,256]{3,2,1,0:T(8,128)(2,1)S(1)}, u32[]{:S(2)}, u32[]{:S(2)}) collective-permute-start(bf16[8,18,8,256]{3,2,1,0:T(8,128)(2,1)S(1)} %collective-permute-done), channel_id=1, source_target_pairs={{0,1},{1,0},{2,3},{3,2},{4,5},{5,4},{6,7},{7,6},{8,9},{9,8},{10,11... | collective-permute-start | bytes 1769480 | tf_op jit(solution)/shard_map/ppermute | solution.py:204
  89.9 38.9 %collective-permute-start.16 = (bf16[128,2304]{1,0:T(8,128)(2,1)S(1)}, bf16[128,2304]{1,0:T(8,128)(2,1)S(1)}, u32[]{:S(2)}, u32[]{:S(2)}) collective-permute-start(bf16[128,2304]{1,0:T(8,128)(2,1)S(1)} %collective-permute-done.14.refs_12_), channel_id=1, source_target_pairs={{0,64},{64,128},{128,192},{192,256},{256,320},{320,384},{384,448},... | collective-permute-start | bytes 1769480 | tf_op jit(solution)/shard_map/ppermute | solution.py:135
  94.6 22.7 %collective-permute-start.15 = (bf16[128,2304]{1,0:T(8,128)(2,1)S(1)}, bf16[128,2304]{1,0:T(8,128)(2,1)S(1)}, u32[]{:S(2)}, u32[]{:S(2)}) collective-permute-start(bf16[128,2304]{1,0:T(8,128)(2,1)S(1)} %collective-permute-done.13.refs_11_), channel_id=1, source_target_pairs={{0,448},{64,0},{128,64},{192,128},{256,192},{320,256},{384,320},{4... | collective-permute-start | bytes 1769480 | tf_op jit(solution)/shard_map/ppermute | solution.py:139
  101.6 24.4 %collective-permute-start.9 = (bf16[128,2304]{1,0:T(8,128)(2,1)S(1)}, bf16[128,2304]{1,0:T(8,128)(2,1)S(1)}, u32[]{:S(2)}, u32[]{:S(2)}) collective-permute-start(bf16[128,2304]{1,0:T(8,128)(2,1)S(1)} %collective-permute-done.8.refs_6_), channel_id=1, source_target_pairs={{0,64},{64,128},{128,192},{192,256},{256,320},{320,384},{384,448},... | collective-permute-start | bytes 1769480 | tf_op jit(solution)/shard_map/ppermute | solution.py:135
  141.4 23.8 %collective-permute-start.18 = (bf16[2,144,2048]{2,1,0:T(8,128)(2,1)S(1)}, bf16[2,144,2048]{2,1,0:T(8,128)(2,1)S(1)}, u32[]{:S(2)}, u32[]{:S(2)}) collective-permute-start(bf16[2,144,2048]{2,1,0:T(8,128)(2,1)S(1)} %get-tuple-element.15), channel_id=1, source_target_pairs={{0,1},{1,0},{2,3},{3,2},{4,5},{5,4},{6,7},{7,6},{8,9},{9,8},{10,11... | collective-permute-start | bytes 3538952 | tf_op jit(solution)/shard_map/ppermute | solution.py:211
  165.7 16.6 %collective-permute-start.19 = (bf16[2,72,2048]{2,1,0:T(8,128)(2,1)S(1)}, bf16[2,72,2048]{2,1,0:T(8,128)(2,1)S(1)}, u32[]{:S(2)}, u32[]{:S(2)}) collective-permute-start(bf16[2,72,2048]{2,1,0:T(8,128)(2,1)S(1)} %slice_bitcast_fusion), channel_id=1, source_target_pairs={{0,2},{2,0},{1,3},{3,1},{4,6},{6,4},{5,7},{7,5},{8,10},{10,8},{9,1... | collective-permute-start | bytes 1769480 | tf_op jit(solution)/shard_map/ppermute | solution.py:213
  171.5 31.2 %collective-permute-start.26 = (bf16[256,768]{1,0:T(8,128)(2,1)S(1)}, bf16[256,768]{1,0:T(8,128)(2,1)S(1)}, u32[]{:S(2)}, u32[]{:S(2)}) collective-permute-start(bf16[256,768]{1,0:T(8,128)(2,1)S(1)} %add_convert_fusion.1), channel_id=1, source_target_pairs={{0,448},{64,0},{128,64},{192,128},{256,192},{320,256},{384,320},{4... | collective-permute-start | bytes 1179656 | tf_op jit(solution)/shard_map/ppermute | solution.py:139
  177.2 25.5 %collective-permute-start.23 = (bf16[256,768]{1,0:T(8,128)(2,1)S(1)}, bf16[256,768]{1,0:T(8,128)(2,1)S(1)}, u32[]{:S(2)}, u32[]{:S(2)}) collective-permute-start(bf16[256,768]{1,0:T(8,128)(2,1)S(1)} %add_convert_fusion.3), channel_id=1, source_target_pairs={{0,64},{64,128},{128,192},{192,256},{256,320},{320,384},{384,448},... | collective-permute-start | bytes 1179656 | tf_op jit(solution)/shard_map/ppermute | solution.py:135
  183.5 42.4 %all-to-all-start.1 = ((bf16[8,18,8,256]{3,2,1,0:T(8,128)(2,1)}), bf16[8,18,8,256]{3,2,1,0:T(8,128)(2,1)S(1)}, u32[]{:S(2)}, u32[]{:S(2)}) async-start(bf16[8,18,8,256]{3,2,1,0:T(8,128)(2,1)} %pad_maximum_fusion.2), calls=%async_computation.1 | async-start | bytes 1179648 | tf_op jit(solution)/shard_map/all_to_all | solution.py:215
  202.9 16.2 %collective-permute-start.27 = (bf16[128,768]{1,0:T(8,128)(2,1)S(1)}, bf16[128,768]{1,0:T(8,128)(2,1)S(1)}, u32[]{:S(2)}, u32[]{:S(2)}) collective-permute-start(bf16[128,768]{1,0:T(8,128)(2,1)S(1)} %slice.585), channel_id=1, source_target_pairs={{0,32},{32,0},{1,33},{33,1},{2,34},{34,2},{3,35},{35,3},{4,36},{36... | collective-permute-start | bytes 589832 | tf_op jit(solution)/shard_map/ppermute | solution.py:227
  (9 other events, 112.9 us)

commit v3 on v2

--- a/solution.py
+++ b/solution.py
@@ -25,7 +25,7 @@
 
 
 HALF = D // 2
-PARTIAL_FLOPS = 30_000_000_000
+PARTIAL_FLOPS = 5_000_000_000
 
 
 def pair(pieces, p, at, width):
@@ -181,24 +181,25 @@
     )
     picked = jnp.dot(pick, both, preferred_element_type=F32)
     a[0] = own
+    routed_x = picked[:, :D].astype(BF)
+    routed_y = (picked[:, D:] * scale[:, None]).astype(BF)
+
+    def fold(v, lead):
+        return v.reshape(lead, CAP, 8, 256)
+
+    payload = jnp.concatenate([fold(routed_x, EXPERTS), fold(routed_y, EXPERTS)], axis=1)
     for s in range(1, 5):
         a[NZ - s] = right(a[(NZ - s + 1) % NZ])
         if s < 4:
             a[s] = left(a[s - 1])
+        if s == 2:
+            payload, b[0], a[2], a[6] = lax.optimization_barrier((payload, b[0], a[2], a[6]))
     for s in range(1, 5):
         if s < 4:
             b[NZ - s] = right(b[(NZ - s + 1) % NZ])
         b[s] = left(b[s - 1])
     mine = [a[k] for k in ORDER]
     pieces = mine + [b[k] for k in ORDER]
-
-    routed_x = picked[:, :D].astype(BF)
-    routed_y = (picked[:, D:] * scale[:, None]).astype(BF)
-
-    def fold(v, lead):
-        return v.reshape(lead, CAP, 8, 256)
-
-    payload = jnp.concatenate([fold(routed_x, EXPERTS), fold(routed_y, EXPERTS)], axis=1)
     block = lax.all_to_all(payload, GROUP, 0, 0, tiled=True)
     beside = lax.ppermute(block, "l", SWAP)
     quarters = (block, beside, lax.ppermute(block, "c", SWAP), lax.ppermute(beside, "c", SWAP))

time: 231 us -> 223 us (0.965)
  starting transfers between devices: 130 us -> 116 us
  waiting for transfers between devices: 73 us -> 78.1 us
    all_to_all x1, starting transfers between devices: 19.2 us -> 7.49 us  [per_device(): got = lax.all_to_all(payload, GROUP, 0, 0, tiled=True)]
    ppermute x11, waiting for transfers between devices: 17.8 us -> 25.3 us  [right(): return lax.ppermute(v, 'z', RIGHT)]
    ppermute x1, waiting for transfers between devices: 6.78 us -> 13.7 us  [per_device(): b[0] = lax.ppermute(own, 'h', SWAP)]
    ppermute x10, waiting for transfers between devices: 27.5 us -> 22.8 us  [left(): return lax.ppermute(v, 'z', LEFT)]
    ppermute x10, starting transfers between devices: 57.5 us -> 53.1 us  [left(): return lax.ppermute(v, 'z', LEFT)]
    ppermute x1, starting transfers between devices: 2.93 us -> 6.83 us  [per_device(): b[0] = lax.ppermute(own, 'h', SWAP)]
    all_to_all x1, starting transfers between devices: 9.89 us -> 6.89 us  [per_device(): block = lax.all_to_all(payload, GROUP, 0, 0, tiled=True)]
  transfers between devices with their start and end apart: 30 -> 30, of which waited for: 14 -> 14; matrix products, arithmetic and copies ran while one was open for 2% -> 4% of each run, Pallas kernels for 1% -> 1%
where the time goes in v3:
time: 223 us; the launch traced here: 222 us
  starting transfers between devices  116 us (52%)
  waiting for transfers between devices  78.1 us (35%)
  Pallas kernels  10.8 us (5%)
  other arithmetic  8.18 us (4%)
  local copies, waits for them, and re-layouts  6.24 us (3%)
    ppermute x10, starting transfers between devices, left(): return lax.ppermute(v, 'z', LEFT)  53.1 us
    ppermute x11, waiting for transfers between devices, right(): return lax.ppermute(v, 'z', RIGHT)  25.3 us
    ppermute x11, starting transfers between devices, right(): return lax.ppermute(v, 'z', RIGHT)  24.2 us
    ppermute x10, waiting for transfers between devices, left(): return lax.ppermute(v, 'z', LEFT)  22.8 us
    ppermute x1, waiting for transfers between devices, per_device(): b[0] = lax.ppermute(own, 'h', SWAP)  13.7 us
    ppermute x1, waiting for transfers between devices, per_device(): crossed = lax.ppermute(near[128:].astype(BF), 'h', SWAP)  9.88 us
    all_to_all x1, starting transfers between devices, per_device(): got = lax.all_to_all(payload, GROUP, 0, 0, tiled=True)  7.49 us
    all_to_all x1, starting transfers between devices, per_device(): block = lax.all_to_all(payload, GROUP, 0, 0, tiled=True)  6.89 us
  transfers between devices with their start and end apart: 30, of which 14 were waited for; matrix products, arithmetic and copies ran while one was open for 4% of the time, Pallas kernels for 1%

profile of v3, /device:TPU:8, one launch (start us, length us, event | category | flops | bytes accessed | tf_op | source)
XLA Modules:
  0.0 221.5 jit_solution(1545674240993535924)
XLA Ops:
  2.8 4.3 %collective-permute-start.3 = (bf16[128,2304]{1,0:T(8,128)(2,1)S(1)}, bf16[128,2304]{1,0:T(8,128)(2,1)S(1)}, u32[]{:S(2)}, u32[]{:S(2)}) collective-permute-start(bf16[128,2304]{1,0:T(8,128)(2,1)S(1)} %pad_maximum_fusion.1.refs_0_), channel_id=1, source_target_pairs={{0,64},{64,128},{128,192},{192,256},{256,320},{320,384},{384,448},... | collective-permute-start | bytes 1769480 | tf_op jit(solution)/shard_map/ppermute | solution.py:135
  7.1 8.6 %collective-permute-start.1 = (bf16[128,2304]{1,0:T(8,128)(2,1)S(1)}, bf16[128,2304]{1,0:T(8,128)(2,1)S(1)}, u32[]{:S(2)}, u32[]{:S(2)}) collective-permute-start(bf16[128,2304]{1,0:T(8,128)(2,1)S(1)} %pad_maximum_fusion.1.refs_0_), channel_id=1, source_target_pairs={{0,448},{64,0},{128,64},{192,128},{256,192},{320,256},{384,320},{4... | collective-permute-start | bytes 1769480 | tf_op jit(solution)/shard_map/ppermute | solution.py:139
  15.7 6.8 %collective-permute-start = (bf16[128,2304]{1,0:T(8,128)(2,1)S(1)}, bf16[128,2304]{1,0:T(8,128)(2,1)S(1)}, u32[]{:S(2)}, u32[]{:S(2)}) collective-permute-start(bf16[128,2304]{1,0:T(8,128)(2,1)S(1)} %pad_maximum_fusion.1.refs_0_), channel_id=1, source_target_pairs={{0,32},{32,0},{1,33},{33,1},{2,34},{34,2},{3,35},{35,3},{4,36},{36... | collective-permute-start | bytes 1769480 | tf_op jit(solution)/shard_map/ppermute | solution.py:166
  29.0 5.1 %collective-permute-start.2 = (bf16[128,2304]{1,0:T(8,128)(2,1)S(1)}, bf16[128,2304]{1,0:T(8,128)(2,1)S(1)}, u32[]{:S(2)}, u32[]{:S(2)}) collective-permute-start(bf16[128,2304]{1,0:T(8,128)(2,1)S(1)} %collective-permute-done.1.refs_1_), channel_id=1, source_target_pairs={{0,448},{64,0},{128,64},{192,128},{256,192},{320,256},{384,320},{4... | collective-permute-start | bytes 1769480 | tf_op jit(solution)/shard_map/ppermute | solution.py:139
  35.2 13.7 %collective-permute-done.refs_8_ = bf16[128,2304]{1,0:T(8,128)(2,1)S(1)} collective-permute-done((bf16[128,2304]{1,0:T(8,128)(2,1)S(1)}, bf16[128,2304]{1,0:T(8,128)(2,1)S(1)}, u32[]{:S(2)}, u32[]{:S(2)}) %collective-permute-start) | collective-permute-done | bytes 589856 | tf_op jit(solution)/shard_map/ppermute | solution.py:166
  49.0 6.9 %all-to-all-start = ((bf16[8,18,8,256]{3,2,1,0:T(8,128)(2,1)}), bf16[8,18,8,256]{3,2,1,0:T(8,128)(2,1)}, u32[]{:S(2)}, u32[]{:S(2)}) async-start(bf16[8,18,8,256]{3,2,1,0:T(8,128)(2,1)} %pad_maximum_fusion), calls=%async_computation | async-start | bytes 1179648 | tf_op jit(solution)/shard_map/all_to_all | solution.py:203
  57.8 5.1 %collective-permute-start.11 = (bf16[128,2304]{1,0:T(8,128)(2,1)S(1)}, bf16[128,2304]{1,0:T(8,128)(2,1)}, u32[]{:S(2)}, u32[]{:S(2)}) collective-permute-start(bf16[128,2304]{1,0:T(8,128)(2,1)S(1)} %collective-permute-done.refs_8_), channel_id=1, source_target_pairs={{0,448},{64,0},{128,64},{192,128},{256,192},{320,256},{384,320},{4... | collective-permute-start | bytes 1769480 | tf_op jit(solution)/shard_map/ppermute | solution.py:139
  64.8 10.5 %collective-permute-done.12.refs_10_ = bf16[128,2304]{1,0:T(8,128)(2,1)} collective-permute-done((bf16[128,2304]{1,0:T(8,128)(2,1)S(1)}, bf16[128,2304]{1,0:T(8,128)(2,1)}, u32[]{:S(2)}, u32[]{:S(2)}) %collective-permute-start.12) | collective-permute-done | bytes 589856 | tf_op jit(solution)/shard_map/ppermute | solution.py:135
  77.2 5.1 %collective-permute-start.13 = (bf16[128,2304]{1,0:T(8,128)(2,1)}, bf16[128,2304]{1,0:T(8,128)(2,1)}, u32[]{:S(2)}, u32[]{:S(2)}) collective-permute-start(bf16[128,2304]{1,0:T(8,128)(2,1)} %collective-permute-done.11.refs_9_), channel_id=1, source_target_pairs={{0,448},{64,0},{128,64},{192,128},{256,192},{320,256},{384,320},{4... | collective-permute-start | bytes 1769480 | tf_op jit(solution)/shard_map/ppermute | solution.py:139
  90.4 8.5 %collective-permute-done.14.refs_12_ = bf16[128,2304]{1,0:T(8,128)(2,1)} collective-permute-done((bf16[128,2304]{1,0:T(8,128)(2,1)}, bf16[128,2304]{1,0:T(8,128)(2,1)}, u32[]{:S(2)}, u32[]{:S(2)}) %collective-permute-start.14) | collective-permute-done | bytes 589856 | tf_op jit(solution)/shard_map/ppermute | solution.py:135
  102.7 5.1 %collective-permute-start.15 = (bf16[128,2304]{1,0:T(8,128)(2,1)}, bf16[128,2304]{1,0:T(8,128)(2,1)S(1)}, u32[]{:S(2)}, u32[]{:S(2)}) collective-permute-start(bf16[128,2304]{1,0:T(8,128)(2,1)} %collective-permute-done.13.refs_11_), channel_id=1, source_target_pairs={{0,448},{64,0},{128,64},{192,128},{256,192},{320,256},{384,320},{4... | collective-permute-start | bytes 1769480 | tf_op jit(solution)/shard_map/ppermute | solution.py:139
  110.3 8.7 %collective-permute-done.15.refs_13_ = bf16[128,2304]{1,0:T(8,128)(2,1)S(1)} collective-permute-done((bf16[128,2304]{1,0:T(8,128)(2,1)}, bf16[128,2304]{1,0:T(8,128)(2,1)S(1)}, u32[]{:S(2)}, u32[]{:S(2)}) %collective-permute-start.15) | collective-permute-done | bytes 589856 | tf_op jit(solution)/shard_map/ppermute | solution.py:139
  119.0 5.5 %collective-permute-start.17 = (bf16[128,2304]{1,0:T(8,128)(2,1)S(1)}, bf16[128,2304]{1,0:T(8,128)(2,1)S(1)}, u32[]{:S(2)}, u32[]{:S(2)}) collective-permute-start(bf16[128,2304]{1,0:T(8,128)(2,1)S(1)} %collective-permute-done.15.refs_13_), channel_id=1, source_target_pairs={{0,448},{64,0},{128,64},{192,128},{256,192},{320,256},{384,320},{4... | collective-permute-start | bytes 1769480 | tf_op jit(solution)/shard_map/ppermute | solution.py:139
  128.4 6.0 %collective-permute-done.17.refs_15_ = bf16[128,2304]{1,0:T(8,128)(2,1)S(1)} collective-permute-done((bf16[128,2304]{1,0:T(8,128)(2,1)S(1)}, bf16[128,2304]{1,0:T(8,128)(2,1)S(1)}, u32[]{:S(2)}, u32[]{:S(2)}) %collective-permute-start.17) | collective-permute-done | bytes 589856 | tf_op jit(solution)/shard_map/ppermute | solution.py:139
  134.4 6.3 %shard_map.95 = (bf16[2,144,2048]{2,1,0:T(8,128)(2,1)S(1)}, bf16[2,144,2048]{2,1,0:T(8,128)(2,1)S(1)}, bf16[288,1536]{1,0:T(8,128)(2,1)S(1)}) custom-call(bf16[288,2048]{1,0:T(8,128)(2,1)S(1)} %constant_dynamic-update-slice_fusion.32.x_ref, bf16[288,2048]{1,0:T(8,128)(2,1)S(1)} %constant_dynamic-update-slice_fusion.36.y_ref, ...), custom_call_target="tpu_custom_call" | custom-call | flops 2717908992 | bytes 20000000 | tf_op jit(solution)/shard_map/pallas_call | solution.py:112
  147.0 5.0 %collective-permute-start.24 = (bf16[256,768]{1,0:T(8,128)(2,1)S(1)}, bf16[256,768]{1,0:T(8,128)(2,1)S(1)}, u32[]{:S(2)}, u32[]{:S(2)}) collective-permute-start(bf16[256,768]{1,0:T(8,128)(2,1)S(1)} %get-tuple-element.29), channel_id=1, source_target_pairs={{0,448},{64,0},{128,64},{192,128},{256,192},{320,256},{384,320},{4... | collective-permute-start | bytes 1179656 | tf_op jit(solution)/shard_map/ppermute | solution.py:139
  155.9 5.1 %collective-permute-done.24 = bf16[256,768]{1,0:T(8,128)(2,1)S(1)} collective-permute-done((bf16[256,768]{1,0:T(8,128)(2,1)S(1)}, bf16[256,768]{1,0:T(8,128)(2,1)S(1)}, u32[]{:S(2)}, u32[]{:S(2)}) %collective-permute-start.24) | collective-permute-done | bytes 393248 | tf_op jit(solution)/shard_map/ppermute | solution.py:139
  161.1 5.6 %collective-permute-start.25 = (bf16[256,768]{1,0:T(8,128)(2,1)S(1)}, bf16[256,768]{1,0:T(8,128)(2,1)S(1)}, u32[]{:S(2)}, u32[]{:S(2)}) collective-permute-start(bf16[256,768]{1,0:T(8,128)(2,1)S(1)} %add_convert_fusion.2), channel_id=1, source_target_pairs={{0,448},{64,0},{128,64},{192,128},{256,192},{320,256},{384,320},{4... | collective-permute-start | bytes 1179656 | tf_op jit(solution)/shard_map/ppermute | solution.py:139
  172.0 3.0 %collective-permute-done.25 = bf16[256,768]{1,0:T(8,128)(2,1)S(1)} collective-permute-done((bf16[256,768]{1,0:T(8,128)(2,1)S(1)}, bf16[256,768]{1,0:T(8,128)(2,1)S(1)}, u32[]{:S(2)}, u32[]{:S(2)}) %collective-permute-start.25) | collective-permute-done | bytes 393248 | tf_op jit(solution)/shard_map/ppermute | solution.py:139
  175.8 5.6 %collective-permute-start.26 = (bf16[256,768]{1,0:T(8,128)(2,1)}, bf16[256,768]{1,0:T(8,128)(2,1)}, u32[]{:S(2)}, u32[]{:S(2)}) collective-permute-start(bf16[256,768]{1,0:T(8,128)(2,1)} %add_convert_fusion.1), channel_id=1, source_target_pairs={{0,448},{64,0},{128,64},{192,128},{256,192},{320,256},{384,320},{4... | collective-permute-start | bytes 1179656 | tf_op jit(solution)/shard_map/ppermute | solution.py:139
  187.3 7.5 %all-to-all-start.1 = ((bf16[8,18,8,256]{3,2,1,0:T(8,128)(2,1)}), bf16[8,18,8,256]{3,2,1,0:T(8,128)(2,1)S(1)}, u32[]{:S(2)}, u32[]{:S(2)}) async-start(bf16[8,18,8,256]{3,2,1,0:T(8,128)(2,1)} %pad_maximum_fusion.2), calls=%async_computation.1 | async-start | bytes 1179648 | tf_op jit(solution)/shard_map/all_to_all | solution.py:216
  196.5 6.3 %collective-permute-start.27 = (bf16[128,768]{1,0:T(8,128)(2,1)S(1)}, bf16[128,768]{1,0:T(8,128)(2,1)S(1)}, u32[]{:S(2)}, u32[]{:S(2)}) collective-permute-start(bf16[128,768]{1,0:T(8,128)(2,1)S(1)} %slice.585), channel_id=1, source_target_pairs={{0,32},{32,0},{1,33},{33,1},{2,34},{34,2},{3,35},{35,3},{4,36},{36... | collective-permute-start | bytes 589832 | tf_op jit(solution)/shard_map/ppermute | solution.py:228
  202.8 9.9 %collective-permute-done.27 = bf16[128,768]{1,0:T(8,128)(2,1)S(1)} collective-permute-done((bf16[128,768]{1,0:T(8,128)(2,1)S(1)}, bf16[128,768]{1,0:T(8,128)(2,1)S(1)}, u32[]{:S(2)}, u32[]{:S(2)}) %collective-permute-start.27) | collective-permute-done | bytes 196640 | tf_op jit(solution)/shard_map/ppermute | solution.py:228
  213.4 4.6 %all-to-all-done.1 = bf16[8,18,8,256]{3,2,1,0:T(8,128)(2,1)S(1)} async-done(((bf16[8,18,8,256]{3,2,1,0:T(8,128)(2,1)}), bf16[8,18,8,256]{3,2,1,0:T(8,128)(2,1)S(1)}, u32[]{:S(2)}, u32[]{:S(2)}) %all-to-all-start.1) | async-done | bytes 589856 | tf_op jit(solution)/shard_map/all_to_all | solution.py:216
  (188 shorter events, 61.0 us)
Async XLA Ops:
  2.8 24.3 %collective-permute-start.3 = (bf16[128,2304]{1,0:T(8,128)(2,1)S(1)}, bf16[128,2304]{1,0:T(8,128)(2,1)S(1)}, u32[]{:S(2)}, u32[]{:S(2)}) collective-permute-start(bf16[128,2304]{1,0:T(8,128)(2,1)S(1)} %pad_maximum_fusion.1.refs_0_), channel_id=1, source_target_pairs={{0,64},{64,128},{128,192},{192,256},{256,320},{320,384},{384,448},... | collective-permute-start | bytes 1769480 | tf_op jit(solution)/shard_map/ppermute | solution.py:135
  7.1 21.9 %collective-permute-start.1 = (bf16[128,2304]{1,0:T(8,128)(2,1)S(1)}, bf16[128,2304]{1,0:T(8,128)(2,1)S(1)}, u32[]{:S(2)}, u32[]{:S(2)}) collective-permute-start(bf16[128,2304]{1,0:T(8,128)(2,1)S(1)} %pad_maximum_fusion.1.refs_0_), channel_id=1, source_target_pairs={{0,448},{64,0},{128,64},{192,128},{256,192},{320,256},{384,320},{4... | collective-permute-start | bytes 1769480 | tf_op jit(solution)/shard_map/ppermute | solution.py:139
  15.7 33.2 %collective-permute-start = (bf16[128,2304]{1,0:T(8,128)(2,1)S(1)}, bf16[128,2304]{1,0:T(8,128)(2,1)S(1)}, u32[]{:S(2)}, u32[]{:S(2)}) collective-permute-start(bf16[128,2304]{1,0:T(8,128)(2,1)S(1)} %pad_maximum_fusion.1.refs_0_), channel_id=1, source_target_pairs={{0,32},{32,0},{1,33},{33,1},{2,34},{34,2},{3,35},{35,3},{4,36},{36... | collective-permute-start | bytes 1769480 | tf_op jit(solution)/shard_map/ppermute | solution.py:166
  27.1 21.8 %collective-permute-start.4 = (bf16[128,2304]{1,0:T(8,128)(2,1)S(1)}, bf16[128,2304]{1,0:T(8,128)(2,1)S(1)}, u32[]{:S(2)}, u32[]{:S(2)}) collective-permute-start(bf16[128,2304]{1,0:T(8,128)(2,1)S(1)} %collective-permute-done.3.refs_2_), channel_id=1, source_target_pairs={{0,64},{64,128},{128,192},{192,256},{256,320},{320,384},{384,448},... | collective-permute-start | bytes 1769480 | tf_op jit(solution)/shard_map/ppermute | solution.py:135
  29.0 19.9 %collective-permute-start.2 = (bf16[128,2304]{1,0:T(8,128)(2,1)S(1)}, bf16[128,2304]{1,0:T(8,128)(2,1)S(1)}, u32[]{:S(2)}, u32[]{:S(2)}) collective-permute-start(bf16[128,2304]{1,0:T(8,128)(2,1)S(1)} %collective-permute-done.1.refs_1_), channel_id=1, source_target_pairs={{0,448},{64,0},{128,64},{192,128},{256,192},{320,256},{384,320},{4... | collective-permute-start | bytes 1769480 | tf_op jit(solution)/shard_map/ppermute | solution.py:139
  49.0 33.4 %all-to-all-start = ((bf16[8,18,8,256]{3,2,1,0:T(8,128)(2,1)}), bf16[8,18,8,256]{3,2,1,0:T(8,128)(2,1)}, u32[]{:S(2)}, u32[]{:S(2)}) async-start(bf16[8,18,8,256]{3,2,1,0:T(8,128)(2,1)} %pad_maximum_fusion), calls=%async_computation | async-start | bytes 1179648 | tf_op jit(solution)/shard_map/all_to_all | solution.py:203
  55.8 19.5 %collective-permute-start.12 = (bf16[128,2304]{1,0:T(8,128)(2,1)S(1)}, bf16[128,2304]{1,0:T(8,128)(2,1)}, u32[]{:S(2)}, u32[]{:S(2)}) collective-permute-start(bf16[128,2304]{1,0:T(8,128)(2,1)S(1)} %collective-permute-done.refs_8_), channel_id=1, source_target_pairs={{0,64},{64,128},{128,192},{192,256},{256,320},{320,384},{384,448},... | collective-permute-start | bytes 1769480 | tf_op jit(solution)/shard_map/ppermute | solution.py:135
  57.8 19.5 %collective-permute-start.11 = (bf16[128,2304]{1,0:T(8,128)(2,1)S(1)}, bf16[128,2304]{1,0:T(8,128)(2,1)}, u32[]{:S(2)}, u32[]{:S(2)}) collective-permute-start(bf16[128,2304]{1,0:T(8,128)(2,1)S(1)} %collective-permute-done.refs_8_), channel_id=1, source_target_pairs={{0,448},{64,0},{128,64},{192,128},{256,192},{320,256},{384,320},{4... | collective-permute-start | bytes 1769480 | tf_op jit(solution)/shard_map/ppermute | solution.py:139
  62.9 25.2 %collective-permute-start.9 = (bf16[128,2304]{1,0:T(8,128)(2,1)S(1)}, bf16[128,2304]{1,0:T(8,128)(2,1)}, u32[]{:S(2)}, u32[]{:S(2)}) collective-permute-start(bf16[128,2304]{1,0:T(8,128)(2,1)S(1)} %collective-permute-done.4.refs_4_), channel_id=1, source_target_pairs={{0,64},{64,128},{128,192},{192,256},{256,320},{320,384},{384,448},... | collective-permute-start | bytes 1769480 | tf_op jit(solution)/shard_map/ppermute | solution.py:135
  75.3 23.5 %collective-permute-start.14 = (bf16[128,2304]{1,0:T(8,128)(2,1)}, bf16[128,2304]{1,0:T(8,128)(2,1)}, u32[]{:S(2)}, u32[]{:S(2)}) collective-permute-start(bf16[128,2304]{1,0:T(8,128)(2,1)} %collective-permute-done.12.refs_10_), channel_id=1, source_target_pairs={{0,64},{64,128},{128,192},{192,256},{256,320},{320,384},{384,448},... | collective-permute-start | bytes 1769480 | tf_op jit(solution)/shard_map/ppermute | solution.py:135
  77.2 23.5 %collective-permute-start.13 = (bf16[128,2304]{1,0:T(8,128)(2,1)}, bf16[128,2304]{1,0:T(8,128)(2,1)}, u32[]{:S(2)}, u32[]{:S(2)}) collective-permute-start(bf16[128,2304]{1,0:T(8,128)(2,1)} %collective-permute-done.11.refs_9_), channel_id=1, source_target_pairs={{0,448},{64,0},{128,64},{192,128},{256,192},{320,256},{384,320},{4... | collective-permute-start | bytes 1769480 | tf_op jit(solution)/shard_map/ppermute | solution.py:139
  82.4 20.3 %collective-permute-start.6 = (bf16[8,18,8,256]{3,2,1,0:T(8,128)(2,1)}, bf16[8,18,8,256]{3,2,1,0:T(8,128)(2,1)S(1)}, u32[]{:S(2)}, u32[]{:S(2)}) collective-permute-start(bf16[8,18,8,256]{3,2,1,0:T(8,128)(2,1)} %all-to-all-done), channel_id=1, source_target_pairs={{0,1},{1,0},{2,3},{3,2},{4,5},{5,4},{6,7},{7,6},{8,9},{9,8},{10,11... | collective-permute-start | bytes 1769480 | tf_op jit(solution)/shard_map/ppermute | solution.py:205
  85.5 22.6 %collective-permute-start.5 = (bf16[8,18,8,256]{3,2,1,0:T(8,128)(2,1)}, bf16[8,18,8,256]{3,2,1,0:T(8,128)(2,1)S(1)}, u32[]{:S(2)}, u32[]{:S(2)}) collective-permute-start(bf16[8,18,8,256]{3,2,1,0:T(8,128)(2,1)} %all-to-all-done), channel_id=1, source_target_pairs={{0,2},{2,0},{1,3},{3,1},{4,6},{6,4},{5,7},{7,5},{8,10},{10,8},{9,1... | collective-permute-start | bytes 1769480 | tf_op jit(solution)/shard_map/ppermute | solution.py:204
  88.1 36.6 %collective-permute-start.8 = (bf16[128,2304]{1,0:T(8,128)(2,1)S(1)}, bf16[128,2304]{1,0:T(8,128)(2,1)S(1)}, u32[]{:S(2)}, u32[]{:S(2)}) collective-permute-start(bf16[128,2304]{1,0:T(8,128)(2,1)S(1)} %collective-permute-done.2.refs_3_), channel_id=1, source_target_pairs={{0,448},{64,0},{128,64},{192,128},{256,192},{320,256},{384,320},{4... | collective-permute-start | bytes 1769480 | tf_op jit(solution)/shard_map/ppermute | solution.py:139
  98.9 25.9 %collective-permute-start.10 = (bf16[128,2304]{1,0:T(8,128)(2,1)}, bf16[128,2304]{1,0:T(8,128)(2,1)S(1)}, u32[]{:S(2)}, u32[]{:S(2)}) collective-permute-start(bf16[128,2304]{1,0:T(8,128)(2,1)} %collective-permute-done.9.refs_6_), channel_id=1, source_target_pairs={{0,64},{64,128},{128,192},{192,256},{256,320},{320,384},{384,448},... | collective-permute-start | bytes 1769480 | tf_op jit(solution)/shard_map/ppermute | solution.py:135
  100.8 27.6 %collective-permute-start.16 = (bf16[128,2304]{1,0:T(8,128)(2,1)}, bf16[128,2304]{1,0:T(8,128)(2,1)S(1)}, u32[]{:S(2)}, u32[]{:S(2)}) collective-permute-start(bf16[128,2304]{1,0:T(8,128)(2,1)} %collective-permute-done.14.refs_12_), channel_id=1, source_target_pairs={{0,64},{64,128},{128,192},{192,256},{256,320},{320,384},{384,448},... | collective-permute-start | bytes 1769480 | tf_op jit(solution)/shard_map/ppermute | solution.py:135
  102.7 16.3 %collective-permute-start.15 = (bf16[128,2304]{1,0:T(8,128)(2,1)}, bf16[128,2304]{1,0:T(8,128)(2,1)S(1)}, u32[]{:S(2)}, u32[]{:S(2)}) collective-permute-start(bf16[128,2304]{1,0:T(8,128)(2,1)} %collective-permute-done.13.refs_11_), channel_id=1, source_target_pairs={{0,448},{64,0},{128,64},{192,128},{256,192},{320,256},{384,320},{4... | collective-permute-start | bytes 1769480 | tf_op jit(solution)/shard_map/ppermute | solution.py:139
  108.3 16.2 %collective-permute-start.7 = (bf16[8,18,8,256]{3,2,1,0:T(8,128)(2,1)S(1)}, bf16[8,18,8,256]{3,2,1,0:T(8,128)(2,1)S(1)}, u32[]{:S(2)}, u32[]{:S(2)}) collective-permute-start(bf16[8,18,8,256]{3,2,1,0:T(8,128)(2,1)S(1)} %collective-permute-done.5), channel_id=1, source_target_pairs={{0,1},{1,0},{2,3},{3,2},{4,5},{5,4},{6,7},{7,6},{8,9},{9,8},{10,11... | collective-permute-start | bytes 1769480 | tf_op jit(solution)/shard_map/ppermute | solution.py:205
  119.0 15.4 %collective-permute-start.17 = (bf16[128,2304]{1,0:T(8,128)(2,1)S(1)}, bf16[128,2304]{1,0:T(8,128)(2,1)S(1)}, u32[]{:S(2)}, u32[]{:S(2)}) collective-permute-start(bf16[128,2304]{1,0:T(8,128)(2,1)S(1)} %collective-permute-done.15.refs_13_), channel_id=1, source_target_pairs={{0,448},{64,0},{128,64},{192,128},{256,192},{320,256},{384,320},{4... | collective-permute-start | bytes 1769480 | tf_op jit(solution)/shard_map/ppermute | solution.py:139
  145.1 23.9 %collective-permute-start.18 = (bf16[2,144,2048]{2,1,0:T(8,128)(2,1)S(1)}, bf16[2,144,2048]{2,1,0:T(8,128)(2,1)S(1)}, u32[]{:S(2)}, u32[]{:S(2)}) collective-permute-start(bf16[2,144,2048]{2,1,0:T(8,128)(2,1)S(1)} %get-tuple-element.23), channel_id=1, source_target_pairs={{0,1},{1,0},{2,3},{3,2},{4,5},{5,4},{6,7},{7,6},{8,9},{9,8},{10,11... | collective-permute-start | bytes 3538952 | tf_op jit(solution)/shard_map/ppermute | solution.py:212
  169.5 16.6 %collective-permute-start.19 = (bf16[2,72,2048]{2,1,0:T(8,128)(2,1)S(1)}, bf16[2,72,2048]{2,1,0:T(8,128)(2,1)S(1)}, u32[]{:S(2)}, u32[]{:S(2)}) collective-permute-start(bf16[2,72,2048]{2,1,0:T(8,128)(2,1)S(1)} %slice_bitcast_fusion), channel_id=1, source_target_pairs={{0,2},{2,0},{1,3},{3,1},{4,6},{6,4},{5,7},{7,5},{8,10},{10,8},{9,1... | collective-permute-start | bytes 1769480 | tf_op jit(solution)/shard_map/ppermute | solution.py:214
  175.8 18.9 %collective-permute-start.26 = (bf16[256,768]{1,0:T(8,128)(2,1)}, bf16[256,768]{1,0:T(8,128)(2,1)}, u32[]{:S(2)}, u32[]{:S(2)}) collective-permute-start(bf16[256,768]{1,0:T(8,128)(2,1)} %add_convert_fusion.1), channel_id=1, source_target_pairs={{0,448},{64,0},{128,64},{192,128},{256,192},{320,256},{384,320},{4... | collective-permute-start | bytes 1179656 | tf_op jit(solution)/shard_map/ppermute | solution.py:139
  187.3 30.7 %all-to-all-start.1 = ((bf16[8,18,8,256]{3,2,1,0:T(8,128)(2,1)}), bf16[8,18,8,256]{3,2,1,0:T(8,128)(2,1)S(1)}, u32[]{:S(2)}, u32[]{:S(2)}) async-start(bf16[8,18,8,256]{3,2,1,0:T(8,128)(2,1)} %pad_maximum_fusion.2), calls=%async_computation.1 | async-start | bytes 1179648 | tf_op jit(solution)/shard_map/all_to_all | solution.py:216
  196.5 16.2 %collective-permute-start.27 = (bf16[128,768]{1,0:T(8,128)(2,1)S(1)}, bf16[128,768]{1,0:T(8,128)(2,1)S(1)}, u32[]{:S(2)}, u32[]{:S(2)}) collective-permute-start(bf16[128,768]{1,0:T(8,128)(2,1)S(1)} %slice.585), channel_id=1, source_target_pairs={{0,32},{32,0},{1,33},{33,1},{2,34},{34,2},{3,35},{35,3},{4,36},{36... | collective-permute-start | bytes 589832 | tf_op jit(solution)/shard_map/ppermute | solution.py:228
  (10 other events, 146.3 us)

commit v4 on v3

--- a/solution.py
+++ b/solution.py
@@ -228,19 +228,13 @@
     crossed = lax.ppermute(near[128:].astype(BF), "h", SWAP)
     grad_gate = (near[:128] + crossed.astype(F32)).astype(BF)[None]
 
-    total = got.astype(F32)
-    sum_out = total[:, :CAP].reshape(EXPERTS * CAP, D) * scale[:, None]
-    sum_back = total[:, CAP:].reshape(EXPERTS * CAP, D)
-    place = (hit0 | hit1).astype(F32)
-    back = lax.dot_general(
-        place,
-        jnp.concatenate([sum_out, sum_back], axis=1),
-        (((0,), (0,)), ((), ())),
-        precision=lax.Precision.HIGHEST,
-        preferred_element_type=F32,
-    ).astype(BF)
-    layer_out = from_relative(back[:, :D], z, h)
-    grad_tokens = from_relative(back[:, D:], z, h)
+    def combined(rows, **kw):
+        spread = (hit0 | hit1).astype(rows.dtype)
+        return lax.dot_general(spread, rows, (((0,), (0,)), ((), ())), preferred_element_type=F32, **kw).astype(BF)
+
+    sum_out = got[:, :CAP].astype(F32).reshape(EXPERTS * CAP, D) * scale[:, None]
+    layer_out = from_relative(combined(sum_out, precision=lax.Precision.HIGHEST), z, h)
+    grad_tokens = from_relative(combined(got[:, CAP:].reshape(EXPERTS * CAP, D)), z, h)
     return (layer_out, grad_tokens, grad_gate)
 
 

time: 223 us -> 223 us (level)
  transfers between devices with their start and end apart: 30 -> 30, of which waited for: 14 -> 13; matrix products, arithmetic and copies ran while one was open for 4% -> 4% of each run, Pallas kernels for 1% -> 1%
where the time goes in v4:
time: 223 us; the launch traced here: 221 us
  starting transfers between devices  116 us (52%)
  waiting for transfers between devices  79.1 us (35%)
  Pallas kernels  10.8 us (5%)
  other arithmetic  6.54 us (3%)
  local copies, waits for them, and re-layouts  6.03 us (3%)
    ppermute x10, starting transfers between devices, left(): return lax.ppermute(v, 'z', LEFT)  53.1 us
    ppermute x11, waiting for transfers between devices, right(): return lax.ppermute(v, 'z', RIGHT)  24.7 us
    ppermute x11, starting transfers between devices, right(): return lax.ppermute(v, 'z', RIGHT)  24.2 us
    ppermute x10, waiting for transfers between devices, left(): return lax.ppermute(v, 'z', LEFT)  22.8 us
    ppermute x1, waiting for transfers between devices, per_device(): b[0] = lax.ppermute(own, 'h', SWAP)  13.7 us
    ppermute x1, waiting for transfers between devices, per_device(): crossed = lax.ppermute(near[128:].astype(BF), 'h', SWAP)  10.1 us
    all_to_all x1, starting transfers between devices, per_device(): got = lax.all_to_all(payload, GROUP, 0, 0, tiled=True)  7.49 us
    all_to_all x1, starting transfers between devices, per_device(): block = lax.all_to_all(payload, GROUP, 0, 0, tiled=True)  6.89 us
  transfers between devices with their start and end apart: 30, of which 13 were waited for; matrix products, arithmetic and copies ran while one was open for 4% of the time, Pallas kernels for 1%

profile of v4, /device:TPU:8, one launch (start us, length us, event | category | flops | bytes accessed | tf_op | source)
XLA Modules:
  0.0 221.3 jit_solution(7183592989958615903)
XLA Ops:
  2.8 4.3 %collective-permute-start.3 = (bf16[128,2304]{1,0:T(8,128)(2,1)S(1)}, bf16[128,2304]{1,0:T(8,128)(2,1)S(1)}, u32[]{:S(2)}, u32[]{:S(2)}) collective-permute-start(bf16[128,2304]{1,0:T(8,128)(2,1)S(1)} %pad_maximum_fusion.1.refs_0_), channel_id=1, source_target_pairs={{0,64},{64,128},{128,192},{192,256},{256,320},{320,384},{384,448},... | collective-permute-start | bytes 1769480 | tf_op jit(solution)/shard_map/ppermute | solution.py:135
  7.1 8.6 %collective-permute-start.1 = (bf16[128,2304]{1,0:T(8,128)(2,1)S(1)}, bf16[128,2304]{1,0:T(8,128)(2,1)S(1)}, u32[]{:S(2)}, u32[]{:S(2)}) collective-permute-start(bf16[128,2304]{1,0:T(8,128)(2,1)S(1)} %pad_maximum_fusion.1.refs_0_), channel_id=1, source_target_pairs={{0,448},{64,0},{128,64},{192,128},{256,192},{320,256},{384,320},{4... | collective-permute-start | bytes 1769480 | tf_op jit(solution)/shard_map/ppermute | solution.py:139
  15.7 6.8 %collective-permute-start = (bf16[128,2304]{1,0:T(8,128)(2,1)S(1)}, bf16[128,2304]{1,0:T(8,128)(2,1)S(1)}, u32[]{:S(2)}, u32[]{:S(2)}) collective-permute-start(bf16[128,2304]{1,0:T(8,128)(2,1)S(1)} %pad_maximum_fusion.1.refs_0_), channel_id=1, source_target_pairs={{0,32},{32,0},{1,33},{33,1},{2,34},{34,2},{3,35},{35,3},{4,36},{36... | collective-permute-start | bytes 1769480 | tf_op jit(solution)/shard_map/ppermute | solution.py:166
  29.0 5.1 %collective-permute-start.2 = (bf16[128,2304]{1,0:T(8,128)(2,1)S(1)}, bf16[128,2304]{1,0:T(8,128)(2,1)S(1)}, u32[]{:S(2)}, u32[]{:S(2)}) collective-permute-start(bf16[128,2304]{1,0:T(8,128)(2,1)S(1)} %collective-permute-done.1.refs_1_), channel_id=1, source_target_pairs={{0,448},{64,0},{128,64},{192,128},{256,192},{320,256},{384,320},{4... | collective-permute-start | bytes 1769480 | tf_op jit(solution)/shard_map/ppermute | solution.py:139
  35.2 13.7 %collective-permute-done.refs_8_ = bf16[128,2304]{1,0:T(8,128)(2,1)S(1)} collective-permute-done((bf16[128,2304]{1,0:T(8,128)(2,1)S(1)}, bf16[128,2304]{1,0:T(8,128)(2,1)S(1)}, u32[]{:S(2)}, u32[]{:S(2)}) %collective-permute-start) | collective-permute-done | bytes 589856 | tf_op jit(solution)/shard_map/ppermute | solution.py:166
  49.0 6.9 %all-to-all-start = ((bf16[8,18,8,256]{3,2,1,0:T(8,128)(2,1)}), bf16[8,18,8,256]{3,2,1,0:T(8,128)(2,1)}, u32[]{:S(2)}, u32[]{:S(2)}) async-start(bf16[8,18,8,256]{3,2,1,0:T(8,128)(2,1)} %pad_maximum_fusion), calls=%async_computation | async-start | bytes 1179648 | tf_op jit(solution)/shard_map/all_to_all | solution.py:203
  57.8 5.1 %collective-permute-start.11 = (bf16[128,2304]{1,0:T(8,128)(2,1)S(1)}, bf16[128,2304]{1,0:T(8,128)(2,1)}, u32[]{:S(2)}, u32[]{:S(2)}) collective-permute-start(bf16[128,2304]{1,0:T(8,128)(2,1)S(1)} %collective-permute-done.refs_8_), channel_id=1, source_target_pairs={{0,448},{64,0},{128,64},{192,128},{256,192},{320,256},{384,320},{4... | collective-permute-start | bytes 1769480 | tf_op jit(solution)/shard_map/ppermute | solution.py:139
  64.8 10.5 %collective-permute-done.12.refs_10_ = bf16[128,2304]{1,0:T(8,128)(2,1)} collective-permute-done((bf16[128,2304]{1,0:T(8,128)(2,1)S(1)}, bf16[128,2304]{1,0:T(8,128)(2,1)}, u32[]{:S(2)}, u32[]{:S(2)}) %collective-permute-start.12) | collective-permute-done | bytes 589856 | tf_op jit(solution)/shard_map/ppermute | solution.py:135
  77.2 5.1 %collective-permute-start.13 = (bf16[128,2304]{1,0:T(8,128)(2,1)}, bf16[128,2304]{1,0:T(8,128)(2,1)}, u32[]{:S(2)}, u32[]{:S(2)}) collective-permute-start(bf16[128,2304]{1,0:T(8,128)(2,1)} %collective-permute-done.11.refs_9_), channel_id=1, source_target_pairs={{0,448},{64,0},{128,64},{192,128},{256,192},{320,256},{384,320},{4... | collective-permute-start | bytes 1769480 | tf_op jit(solution)/shard_map/ppermute | solution.py:139
  90.4 8.5 %collective-permute-done.14.refs_12_ = bf16[128,2304]{1,0:T(8,128)(2,1)} collective-permute-done((bf16[128,2304]{1,0:T(8,128)(2,1)}, bf16[128,2304]{1,0:T(8,128)(2,1)}, u32[]{:S(2)}, u32[]{:S(2)}) %collective-permute-start.14) | collective-permute-done | bytes 589856 | tf_op jit(solution)/shard_map/ppermute | solution.py:135
  102.7 5.1 %collective-permute-start.15 = (bf16[128,2304]{1,0:T(8,128)(2,1)}, bf16[128,2304]{1,0:T(8,128)(2,1)S(1)}, u32[]{:S(2)}, u32[]{:S(2)}) collective-permute-start(bf16[128,2304]{1,0:T(8,128)(2,1)} %collective-permute-done.13.refs_11_), channel_id=1, source_target_pairs={{0,448},{64,0},{128,64},{192,128},{256,192},{320,256},{384,320},{4... | collective-permute-start | bytes 1769480 | tf_op jit(solution)/shard_map/ppermute | solution.py:139
  110.3 8.7 %collective-permute-done.15.refs_13_ = bf16[128,2304]{1,0:T(8,128)(2,1)S(1)} collective-permute-done((bf16[128,2304]{1,0:T(8,128)(2,1)}, bf16[128,2304]{1,0:T(8,128)(2,1)S(1)}, u32[]{:S(2)}, u32[]{:S(2)}) %collective-permute-start.15) | collective-permute-done | bytes 589856 | tf_op jit(solution)/shard_map/ppermute | solution.py:139
  119.0 5.5 %collective-permute-start.17 = (bf16[128,2304]{1,0:T(8,128)(2,1)S(1)}, bf16[128,2304]{1,0:T(8,128)(2,1)S(1)}, u32[]{:S(2)}, u32[]{:S(2)}) collective-permute-start(bf16[128,2304]{1,0:T(8,128)(2,1)S(1)} %collective-permute-done.15.refs_13_), channel_id=1, source_target_pairs={{0,448},{64,0},{128,64},{192,128},{256,192},{320,256},{384,320},{4... | collective-permute-start | bytes 1769480 | tf_op jit(solution)/shard_map/ppermute | solution.py:139
  128.4 6.0 %collective-permute-done.17.refs_15_ = bf16[128,2304]{1,0:T(8,128)(2,1)S(1)} collective-permute-done((bf16[128,2304]{1,0:T(8,128)(2,1)S(1)}, bf16[128,2304]{1,0:T(8,128)(2,1)S(1)}, u32[]{:S(2)}, u32[]{:S(2)}) %collective-permute-start.17) | collective-permute-done | bytes 589856 | tf_op jit(solution)/shard_map/ppermute | solution.py:139
  134.4 6.3 %shard_map.95 = (bf16[2,144,2048]{2,1,0:T(8,128)(2,1)S(1)}, bf16[2,144,2048]{2,1,0:T(8,128)(2,1)S(1)}, bf16[288,1536]{1,0:T(8,128)(2,1)S(1)}) custom-call(bf16[288,2048]{1,0:T(8,128)(2,1)S(1)} %constant_dynamic-update-slice_fusion.32.x_ref, bf16[288,2048]{1,0:T(8,128)(2,1)S(1)} %constant_dynamic-update-slice_fusion.36.y_ref, ...), custom_call_target="tpu_custom_call" | custom-call | flops 2717908992 | bytes 20000000 | tf_op jit(solution)/shard_map/pallas_call | solution.py:112
  147.0 5.0 %collective-permute-start.24 = (bf16[256,768]{1,0:T(8,128)(2,1)S(1)}, bf16[256,768]{1,0:T(8,128)(2,1)S(1)}, u32[]{:S(2)}, u32[]{:S(2)}) collective-permute-start(bf16[256,768]{1,0:T(8,128)(2,1)S(1)} %get-tuple-element.29), channel_id=1, source_target_pairs={{0,448},{64,0},{128,64},{192,128},{256,192},{320,256},{384,320},{4... | collective-permute-start | bytes 1179656 | tf_op jit(solution)/shard_map/ppermute | solution.py:139
  155.9 5.1 %collective-permute-done.24 = bf16[256,768]{1,0:T(8,128)(2,1)S(1)} collective-permute-done((bf16[256,768]{1,0:T(8,128)(2,1)S(1)}, bf16[256,768]{1,0:T(8,128)(2,1)S(1)}, u32[]{:S(2)}, u32[]{:S(2)}) %collective-permute-start.24) | collective-permute-done | bytes 393248 | tf_op jit(solution)/shard_map/ppermute | solution.py:139
  161.1 5.6 %collective-permute-start.25 = (bf16[256,768]{1,0:T(8,128)(2,1)S(1)}, bf16[256,768]{1,0:T(8,128)(2,1)S(1)}, u32[]{:S(2)}, u32[]{:S(2)}) collective-permute-start(bf16[256,768]{1,0:T(8,128)(2,1)S(1)} %add_convert_fusion.2), channel_id=1, source_target_pairs={{0,448},{64,0},{128,64},{192,128},{256,192},{320,256},{384,320},{4... | collective-permute-start | bytes 1179656 | tf_op jit(solution)/shard_map/ppermute | solution.py:139
  175.1 5.6 %collective-permute-start.26 = (bf16[256,768]{1,0:T(8,128)(2,1)S(1)}, bf16[256,768]{1,0:T(8,128)(2,1)S(1)}, u32[]{:S(2)}, u32[]{:S(2)}) collective-permute-start(bf16[256,768]{1,0:T(8,128)(2,1)S(1)} %add_convert_fusion.1), channel_id=1, source_target_pairs={{0,448},{64,0},{128,64},{192,128},{256,192},{320,256},{384,320},{4... | collective-permute-start | bytes 1179656 | tf_op jit(solution)/shard_map/ppermute | solution.py:139
  182.7 3.3 %collective-permute-done.19 = bf16[2,72,2048]{2,1,0:T(8,128)(2,1)S(1)} collective-permute-done((bf16[2,72,2048]{2,1,0:T(8,128)(2,1)S(1)}, bf16[2,72,2048]{2,1,0:T(8,128)(2,1)S(1)}, u32[]{:S(2)}, u32[]{:S(2)}) %collective-permute-start.19) | collective-permute-done | bytes 589856 | tf_op jit(solution)/shard_map/ppermute | solution.py:214
  187.3 7.5 %all-to-all-start.1 = ((bf16[8,18,8,256]{3,2,1,0:T(8,128)(2,1)}), bf16[8,18,8,256]{3,2,1,0:T(8,128)(2,1)S(1)}, u32[]{:S(2)}, u32[]{:S(2)}) async-start(bf16[8,18,8,256]{3,2,1,0:T(8,128)(2,1)} %pad_maximum_fusion.2), calls=%async_computation.1 | async-start | bytes 1179648 | tf_op jit(solution)/shard_map/all_to_all | solution.py:216
  196.0 6.8 %collective-permute-start.27 = (bf16[128,768]{1,0:T(8,128)(2,1)S(1)}, bf16[128,768]{1,0:T(8,128)(2,1)S(1)}, u32[]{:S(2)}, u32[]{:S(2)}) collective-permute-start(bf16[128,768]{1,0:T(8,128)(2,1)S(1)} %slice.580), channel_id=1, source_target_pairs={{0,32},{32,0},{1,33},{33,1},{2,34},{34,2},{3,35},{35,3},{4,36},{36... | collective-permute-start | bytes 589832 | tf_op jit(solution)/shard_map/ppermute | solution.py:228
  202.8 10.1 %collective-permute-done.27 = bf16[128,768]{1,0:T(8,128)(2,1)S(1)} collective-permute-done((bf16[128,768]{1,0:T(8,128)(2,1)S(1)}, bf16[128,768]{1,0:T(8,128)(2,1)S(1)}, u32[]{:S(2)}, u32[]{:S(2)}) %collective-permute-start.27) | collective-permute-done | bytes 196640 | tf_op jit(solution)/shard_map/ppermute | solution.py:228
  213.6 4.4 %all-to-all-done.1 = bf16[8,18,8,256]{3,2,1,0:T(8,128)(2,1)S(1)} async-done(((bf16[8,18,8,256]{3,2,1,0:T(8,128)(2,1)}), bf16[8,18,8,256]{3,2,1,0:T(8,128)(2,1)S(1)}, u32[]{:S(2)}, u32[]{:S(2)}) %all-to-all-start.1) | async-done | bytes 589856 | tf_op jit(solution)/shard_map/all_to_all | solution.py:216
  (189 shorter events, 59.9 us)
Async XLA Ops:
  2.8 24.3 %collective-permute-start.3 = (bf16[128,2304]{1,0:T(8,128)(2,1)S(1)}, bf16[128,2304]{1,0:T(8,128)(2,1)S(1)}, u32[]{:S(2)}, u32[]{:S(2)}) collective-permute-start(bf16[128,2304]{1,0:T(8,128)(2,1)S(1)} %pad_maximum_fusion.1.refs_0_), channel_id=1, source_target_pairs={{0,64},{64,128},{128,192},{192,256},{256,320},{320,384},{384,448},... | collective-permute-start | bytes 1769480 | tf_op jit(solution)/shard_map/ppermute | solution.py:135
  7.1 21.9 %collective-permute-start.1 = (bf16[128,2304]{1,0:T(8,128)(2,1)S(1)}, bf16[128,2304]{1,0:T(8,128)(2,1)S(1)}, u32[]{:S(2)}, u32[]{:S(2)}) collective-permute-start(bf16[128,2304]{1,0:T(8,128)(2,1)S(1)} %pad_maximum_fusion.1.refs_0_), channel_id=1, source_target_pairs={{0,448},{64,0},{128,64},{192,128},{256,192},{320,256},{384,320},{4... | collective-permute-start | bytes 1769480 | tf_op jit(solution)/shard_map/ppermute | solution.py:139
  15.7 33.2 %collective-permute-start = (bf16[128,2304]{1,0:T(8,128)(2,1)S(1)}, bf16[128,2304]{1,0:T(8,128)(2,1)S(1)}, u32[]{:S(2)}, u32[]{:S(2)}) collective-permute-start(bf16[128,2304]{1,0:T(8,128)(2,1)S(1)} %pad_maximum_fusion.1.refs_0_), channel_id=1, source_target_pairs={{0,32},{32,0},{1,33},{33,1},{2,34},{34,2},{3,35},{35,3},{4,36},{36... | collective-permute-start | bytes 1769480 | tf_op jit(solution)/shard_map/ppermute | solution.py:166
  27.1 21.8 %collective-permute-start.4 = (bf16[128,2304]{1,0:T(8,128)(2,1)S(1)}, bf16[128,2304]{1,0:T(8,128)(2,1)S(1)}, u32[]{:S(2)}, u32[]{:S(2)}) collective-permute-start(bf16[128,2304]{1,0:T(8,128)(2,1)S(1)} %collective-permute-done.3.refs_2_), channel_id=1, source_target_pairs={{0,64},{64,128},{128,192},{192,256},{256,320},{320,384},{384,448},... | collective-permute-start | bytes 1769480 | tf_op jit(solution)/shard_map/ppermute | solution.py:135
  29.0 19.9 %collective-permute-start.2 = (bf16[128,2304]{1,0:T(8,128)(2,1)S(1)}, bf16[128,2304]{1,0:T(8,128)(2,1)S(1)}, u32[]{:S(2)}, u32[]{:S(2)}) collective-permute-start(bf16[128,2304]{1,0:T(8,128)(2,1)S(1)} %collective-permute-done.1.refs_1_), channel_id=1, source_target_pairs={{0,448},{64,0},{128,64},{192,128},{256,192},{320,256},{384,320},{4... | collective-permute-start | bytes 1769480 | tf_op jit(solution)/shard_map/ppermute | solution.py:139
  49.0 33.4 %all-to-all-start = ((bf16[8,18,8,256]{3,2,1,0:T(8,128)(2,1)}), bf16[8,18,8,256]{3,2,1,0:T(8,128)(2,1)}, u32[]{:S(2)}, u32[]{:S(2)}) async-start(bf16[8,18,8,256]{3,2,1,0:T(8,128)(2,1)} %pad_maximum_fusion), calls=%async_computation | async-start | bytes 1179648 | tf_op jit(solution)/shard_map/all_to_all | solution.py:203
  55.8 19.5 %collective-permute-start.12 = (bf16[128,2304]{1,0:T(8,128)(2,1)S(1)}, bf16[128,2304]{1,0:T(8,128)(2,1)}, u32[]{:S(2)}, u32[]{:S(2)}) collective-permute-start(bf16[128,2304]{1,0:T(8,128)(2,1)S(1)} %collective-permute-done.refs_8_), channel_id=1, source_target_pairs={{0,64},{64,128},{128,192},{192,256},{256,320},{320,384},{384,448},... | collective-permute-start | bytes 1769480 | tf_op jit(solution)/shard_map/ppermute | solution.py:135
  57.8 19.5 %collective-permute-start.11 = (bf16[128,2304]{1,0:T(8,128)(2,1)S(1)}, bf16[128,2304]{1,0:T(8,128)(2,1)}, u32[]{:S(2)}, u32[]{:S(2)}) collective-permute-start(bf16[128,2304]{1,0:T(8,128)(2,1)S(1)} %collective-permute-done.refs_8_), channel_id=1, source_target_pairs={{0,448},{64,0},{128,64},{192,128},{256,192},{320,256},{384,320},{4... | collective-permute-start | bytes 1769480 | tf_op jit(solution)/shard_map/ppermute | solution.py:139
  62.9 25.2 %collective-permute-start.9 = (bf16[128,2304]{1,0:T(8,128)(2,1)S(1)}, bf16[128,2304]{1,0:T(8,128)(2,1)}, u32[]{:S(2)}, u32[]{:S(2)}) collective-permute-start(bf16[128,2304]{1,0:T(8,128)(2,1)S(1)} %collective-permute-done.4.refs_4_), channel_id=1, source_target_pairs={{0,64},{64,128},{128,192},{192,256},{256,320},{320,384},{384,448},... | collective-permute-start | bytes 1769480 | tf_op jit(solution)/shard_map/ppermute | solution.py:135
  75.3 23.5 %collective-permute-start.14 = (bf16[128,2304]{1,0:T(8,128)(2,1)}, bf16[128,2304]{1,0:T(8,128)(2,1)}, u32[]{:S(2)}, u32[]{:S(2)}) collective-permute-start(bf16[128,2304]{1,0:T(8,128)(2,1)} %collective-permute-done.12.refs_10_), channel_id=1, source_target_pairs={{0,64},{64,128},{128,192},{192,256},{256,320},{320,384},{384,448},... | collective-permute-start | bytes 1769480 | tf_op jit(solution)/shard_map/ppermute | solution.py:135
  77.2 23.5 %collective-permute-start.13 = (bf16[128,2304]{1,0:T(8,128)(2,1)}, bf16[128,2304]{1,0:T(8,128)(2,1)}, u32[]{:S(2)}, u32[]{:S(2)}) collective-permute-start(bf16[128,2304]{1,0:T(8,128)(2,1)} %collective-permute-done.11.refs_9_), channel_id=1, source_target_pairs={{0,448},{64,0},{128,64},{192,128},{256,192},{320,256},{384,320},{4... | collective-permute-start | bytes 1769480 | tf_op jit(solution)/shard_map/ppermute | solution.py:139
  82.4 20.3 %collective-permute-start.6 = (bf16[8,18,8,256]{3,2,1,0:T(8,128)(2,1)}, bf16[8,18,8,256]{3,2,1,0:T(8,128)(2,1)S(1)}, u32[]{:S(2)}, u32[]{:S(2)}) collective-permute-start(bf16[8,18,8,256]{3,2,1,0:T(8,128)(2,1)} %all-to-all-done), channel_id=1, source_target_pairs={{0,1},{1,0},{2,3},{3,2},{4,5},{5,4},{6,7},{7,6},{8,9},{9,8},{10,11... | collective-permute-start | bytes 1769480 | tf_op jit(solution)/shard_map/ppermute | solution.py:205
  85.5 22.6 %collective-permute-start.5 = (bf16[8,18,8,256]{3,2,1,0:T(8,128)(2,1)}, bf16[8,18,8,256]{3,2,1,0:T(8,128)(2,1)S(1)}, u32[]{:S(2)}, u32[]{:S(2)}) collective-permute-start(bf16[8,18,8,256]{3,2,1,0:T(8,128)(2,1)} %all-to-all-done), channel_id=1, source_target_pairs={{0,2},{2,0},{1,3},{3,1},{4,6},{6,4},{5,7},{7,5},{8,10},{10,8},{9,1... | collective-permute-start | bytes 1769480 | tf_op jit(solution)/shard_map/ppermute | solution.py:204
  88.1 36.6 %collective-permute-start.8 = (bf16[128,2304]{1,0:T(8,128)(2,1)S(1)}, bf16[128,2304]{1,0:T(8,128)(2,1)S(1)}, u32[]{:S(2)}, u32[]{:S(2)}) collective-permute-start(bf16[128,2304]{1,0:T(8,128)(2,1)S(1)} %collective-permute-done.2.refs_3_), channel_id=1, source_target_pairs={{0,448},{64,0},{128,64},{192,128},{256,192},{320,256},{384,320},{4... | collective-permute-start | bytes 1769480 | tf_op jit(solution)/shard_map/ppermute | solution.py:139
  98.9 25.9 %collective-permute-start.10 = (bf16[128,2304]{1,0:T(8,128)(2,1)}, bf16[128,2304]{1,0:T(8,128)(2,1)S(1)}, u32[]{:S(2)}, u32[]{:S(2)}) collective-permute-start(bf16[128,2304]{1,0:T(8,128)(2,1)} %collective-permute-done.9.refs_6_), channel_id=1, source_target_pairs={{0,64},{64,128},{128,192},{192,256},{256,320},{320,384},{384,448},... | collective-permute-start | bytes 1769480 | tf_op jit(solution)/shard_map/ppermute | solution.py:135
  100.8 27.6 %collective-permute-start.16 = (bf16[128,2304]{1,0:T(8,128)(2,1)}, bf16[128,2304]{1,0:T(8,128)(2,1)S(1)}, u32[]{:S(2)}, u32[]{:S(2)}) collective-permute-start(bf16[128,2304]{1,0:T(8,128)(2,1)} %collective-permute-done.14.refs_12_), channel_id=1, source_target_pairs={{0,64},{64,128},{128,192},{192,256},{256,320},{320,384},{384,448},... | collective-permute-start | bytes 1769480 | tf_op jit(solution)/shard_map/ppermute | solution.py:135
  102.7 16.3 %collective-permute-start.15 = (bf16[128,2304]{1,0:T(8,128)(2,1)}, bf16[128,2304]{1,0:T(8,128)(2,1)S(1)}, u32[]{:S(2)}, u32[]{:S(2)}) collective-permute-start(bf16[128,2304]{1,0:T(8,128)(2,1)} %collective-permute-done.13.refs_11_), channel_id=1, source_target_pairs={{0,448},{64,0},{128,64},{192,128},{256,192},{320,256},{384,320},{4... | collective-permute-start | bytes 1769480 | tf_op jit(solution)/shard_map/ppermute | solution.py:139
  108.3 16.2 %collective-permute-start.7 = (bf16[8,18,8,256]{3,2,1,0:T(8,128)(2,1)S(1)}, bf16[8,18,8,256]{3,2,1,0:T(8,128)(2,1)S(1)}, u32[]{:S(2)}, u32[]{:S(2)}) collective-permute-start(bf16[8,18,8,256]{3,2,1,0:T(8,128)(2,1)S(1)} %collective-permute-done.5), channel_id=1, source_target_pairs={{0,1},{1,0},{2,3},{3,2},{4,5},{5,4},{6,7},{7,6},{8,9},{9,8},{10,11... | collective-permute-start | bytes 1769480 | tf_op jit(solution)/shard_map/ppermute | solution.py:205
  119.0 15.4 %collective-permute-start.17 = (bf16[128,2304]{1,0:T(8,128)(2,1)S(1)}, bf16[128,2304]{1,0:T(8,128)(2,1)S(1)}, u32[]{:S(2)}, u32[]{:S(2)}) collective-permute-start(bf16[128,2304]{1,0:T(8,128)(2,1)S(1)} %collective-permute-done.15.refs_13_), channel_id=1, source_target_pairs={{0,448},{64,0},{128,64},{192,128},{256,192},{320,256},{384,320},{4... | collective-permute-start | bytes 1769480 | tf_op jit(solution)/shard_map/ppermute | solution.py:139
  145.1 23.9 %collective-permute-start.18 = (bf16[2,144,2048]{2,1,0:T(8,128)(2,1)S(1)}, bf16[2,144,2048]{2,1,0:T(8,128)(2,1)S(1)}, u32[]{:S(2)}, u32[]{:S(2)}) collective-permute-start(bf16[2,144,2048]{2,1,0:T(8,128)(2,1)S(1)} %get-tuple-element.23), channel_id=1, source_target_pairs={{0,1},{1,0},{2,3},{3,2},{4,5},{5,4},{6,7},{7,6},{8,9},{9,8},{10,11... | collective-permute-start | bytes 3538952 | tf_op jit(solution)/shard_map/ppermute | solution.py:212
  169.5 16.6 %collective-permute-start.19 = (bf16[2,72,2048]{2,1,0:T(8,128)(2,1)S(1)}, bf16[2,72,2048]{2,1,0:T(8,128)(2,1)S(1)}, u32[]{:S(2)}, u32[]{:S(2)}) collective-permute-start(bf16[2,72,2048]{2,1,0:T(8,128)(2,1)S(1)} %slice_bitcast_fusion), channel_id=1, source_target_pairs={{0,2},{2,0},{1,3},{3,1},{4,6},{6,4},{5,7},{7,5},{8,10},{10,8},{9,1... | collective-permute-start | bytes 1769480 | tf_op jit(solution)/shard_map/ppermute | solution.py:214
  175.1 19.7 %collective-permute-start.26 = (bf16[256,768]{1,0:T(8,128)(2,1)S(1)}, bf16[256,768]{1,0:T(8,128)(2,1)S(1)}, u32[]{:S(2)}, u32[]{:S(2)}) collective-permute-start(bf16[256,768]{1,0:T(8,128)(2,1)S(1)} %add_convert_fusion.1), channel_id=1, source_target_pairs={{0,448},{64,0},{128,64},{192,128},{256,192},{320,256},{384,320},{4... | collective-permute-start | bytes 1179656 | tf_op jit(solution)/shard_map/ppermute | solution.py:139
  187.3 30.6 %all-to-all-start.1 = ((bf16[8,18,8,256]{3,2,1,0:T(8,128)(2,1)}), bf16[8,18,8,256]{3,2,1,0:T(8,128)(2,1)S(1)}, u32[]{:S(2)}, u32[]{:S(2)}) async-start(bf16[8,18,8,256]{3,2,1,0:T(8,128)(2,1)} %pad_maximum_fusion.2), calls=%async_computation.1 | async-start | bytes 1179648 | tf_op jit(solution)/shard_map/all_to_all | solution.py:216
  196.0 16.9 %collective-permute-start.27 = (bf16[128,768]{1,0:T(8,128)(2,1)S(1)}, bf16[128,768]{1,0:T(8,128)(2,1)S(1)}, u32[]{:S(2)}, u32[]{:S(2)}) collective-permute-start(bf16[128,768]{1,0:T(8,128)(2,1)S(1)} %slice.580), channel_id=1, source_target_pairs={{0,32},{32,0},{1,33},{33,1},{2,34},{34,2},{3,35},{35,3},{4,36},{36... | collective-permute-start | bytes 589832 | tf_op jit(solution)/shard_map/ppermute | solution.py:228
  (10 other events, 146.6 us)
